TPU v7x, 32 devices: a whole 2x2x4 slice. The times are simulated.
32 devices in a mesh: dp: 8 (over y, x, core), section: 4 (over z).
Axes of the slice: x: 2, y: 2, z: 4, core: 2. Of those that a mesh axis runs over, the one named last changes fastest.
Arguments:
- features: bfloat16 [8192, 1024], P('dp'), may hold values from -6 to 6
- cotangent: bfloat16 [8192, 1024], P('dp'), may hold values from -8 to 8
- row_counts: int32 [8, 8], P('dp'), may hold values from 1 to 512, 1024 in all within a row
- key_valid: int32 [8192], P('dp'), may hold values 0 or 1
- attend_gain: float32 [1024], replicated, may hold values from 0.25 to 1.75
- attend_qkv: bfloat16 [1024, 3072], replicated, may hold values from -0.1875 to 0.1875
- attend_out: bfloat16 [1024, 1024], replicated, may hold values from -1.5 to 1.5
- mixer_gain: float32 [1024], replicated, may hold values from 0.25 to 1.75
- mixer_up: bfloat16 [1024, 4096], replicated, may hold values from -0.1875 to 0.1875
- mixer_down: bfloat16 [4096, 1024], replicated, may hold values from -0.09375 to 0.09375
- column_gain: float32 [64], replicated, may hold values from 0.25 to 1.75
- column_qkv: bfloat16 [64, 192], replicated, may hold values from -0.75 to 0.75
- column_out: bfloat16 [64, 64], replicated, may hold values from -2 to 2
- column_mix_gain: float32 [64], replicated, may hold values from 0.25 to 1.75
- column_up: bfloat16 [64, 256], replicated, may hold values from -0.75 to 0.75
- column_down: bfloat16 [256, 64], replicated, may hold values from -0.375 to 0.375
Outputs:
- result: bfloat16 [8192, 1024], P('dp', 'section')
- input_grad: float32 [8192, 1024], P('dp', 'section')
- attend_gain_grad: float32 [1024], P(('dp', 'section'))
- attend_qkv_grad: float32 [1024, 3072], P(('dp', 'section'))
- attend_out_grad: float32 [1024, 1024], P(('dp', 'section'))
- mixer_gain_grad: float32 [1024], P(('dp', 'section'))
- mixer_up_grad: float32 [1024, 4096], P(('dp', 'section'))
- mixer_down_grad: float32 [4096, 1024], P(('dp', 'section'))
- column_gain_grad: float32 [64], replicated
- column_qkv_grad: float32 [64, 192], replicated
- column_out_grad: float32 [64, 64], replicated
- column_mix_gain_grad: float32 [64], replicated
- column_up_grad: float32 [64, 256], replicated
- column_down_grad: float32 [256, 64], replicated
Inputs may be any that keep to these rules, and one draw needn't show every extreme that they name: `row_counts`: each group's 8 counts sum to 1024, and the largest of each group is exactly 512.
All inputs are finite; a program needn't handle non-finite values. No bound on the sum of `key_valid` on one device may be relied on, other than what follows from the above.
Results may differ from a plain program's by a relative error of at most 0.023.
Values may be sent and summed in bfloat16 or wider, within the bound.
No kernel may reach another device: no remote copies, remote signals or barrier semaphores. Data moves between devices by JAX's collectives and lax.ppermute only.
A program may use at most 384 MiB of HBM per device.

v0:
```python
import jax
import jax.numpy as jnp
from jax import lax
from jax.sharding import PartitionSpec as P

MICRO = 4
ATTR = 16
HEADS = 8
HEADS_ATTR = 8


EPSILON = 1e-05
MASKED = -1e30
GELU_SCALE = 0.7978845608028654


def shortened(x):
    return jax.tree.map(lambda a: a.astype(jnp.bfloat16) if a.dtype == jnp.float32 else a, x)


def passed_along(value, axis, steps):
    count = lax.axis_size(axis)
    leading, last = (max(0, -steps), min(count, count - steps))
    return lax.ppermute(value, axis, [(source, source + steps) for source in range(leading, last)])


def broadcast(value, axis, source):
    kept = jnp.where(lax.axis_index(axis) == source, value, 0).astype(value.dtype)
    return lax.psum(kept, axis)


def normalize(vector, gain_vec):
    centred = vector - jnp.mean(vector, axis=-1, keepdims=True)
    second = jnp.mean(centred * centred, axis=-1, keepdims=True)
    return centred * lax.rsqrt(second + EPSILON) * gain_vec


def normalize_back(vector, gain_vec, upstream):
    _, pullback = jax.vjp(normalize, vector, gain_vec)
    return pullback(upstream)


def smooth(inputs):
    return (
        0.5 * inputs * (1.0 + jnp.tanh(GELU_SCALE * (inputs + 0.044715 * inputs * inputs * inputs)))
    )


def smooth_back(inputs, upstream):
    _, pullback = jax.vjp(smooth, inputs)
    return pullback(upstream)[0]


def contract_rows(left, right):
    return lax.dot_general(
        left, right, (((0,), (0,)), ((), ())), preferred_element_type=jnp.float32
    )


def contract_last(left, right):
    return lax.dot_general(
        left, right, (((1,), (1,)), ((), ())), preferred_element_type=jnp.float32
    )


def add_at(gradients, first, additions):
    count_new = len(additions)
    summed = tuple((old + new for old, new in zip(gradients[first : first + count_new], additions)))
    return gradients[:first] + summed + gradients[first + count_new :]


def mixer_back(widened, gain_vec, up_matrix, down_matrix, upstream):
    normed = normalize(widened, gain_vec).astype(jnp.bfloat16)
    lifted = jnp.dot(normed, up_matrix, preferred_element_type=jnp.float32)
    hidden = smooth(lifted).astype(jnp.bfloat16)
    down_grad = contract_rows(hidden, upstream)
    pulled = contract_last(upstream, down_matrix)
    lifted_grad = smooth_back(lifted, pulled).astype(jnp.bfloat16)
    up_grad = contract_rows(normed, lifted_grad)
    normed_grad = contract_last(lifted_grad, up_matrix)
    widened_grad, gain_grad = normalize_back(widened, gain_vec, normed_grad)
    return (upstream.astype(jnp.float32) + widened_grad, gain_grad, up_grad, down_grad)


def body(
    features,
    cotangent,
    row_counts,
    key_valid,
    attend_gain,
    attend_qkv,
    attend_out,
    mixer_gain,
    mixer_up,
    mixer_down,
    column_gain,
    column_qkv,
    column_out,
    column_mix_gain,
    column_up,
    column_down,
):
    section_count = lax.axis_size("section")
    last_section = section_count - 1
    mesh_at = lax.axis_index("section")
    section_at = last_section - mesh_at
    row_count, model_width = features.shape
    block_rows = row_count // MICRO
    head_count = HEADS
    head_dim = model_width // head_count
    attr_count = ATTR
    embed_width = model_width // attr_count
    small_dim = embed_width // HEADS_ATTR
    scale_big = head_dim ** (-0.5)
    scale_small = small_dim ** (-0.5)
    places = lax.iota(jnp.int32, row_count)
    bounds = jnp.cumsum(row_counts[0])
    segment = jnp.sum((places[:, None] >= bounds[None, :]).astype(jnp.int32), axis=1)
    usable = key_valid == 1
    zero_sums = jnp.zeros((head_count, block_rows), jnp.float32)

    def prepare(inputs):
        normed = normalize(inputs.astype(jnp.float32), attend_gain).astype(jnp.bfloat16)
        projected = jnp.dot(normed, attend_qkv, preferred_element_type=jnp.float32).astype(
            jnp.bfloat16
        )
        return (normed, projected.reshape(row_count, 3, head_count, head_dim).transpose(1, 2, 0, 3))

    def vacant(inputs):
        return (
            jnp.zeros((row_count, model_width), jnp.bfloat16),
            jnp.zeros((3, head_count, row_count, head_dim), jnp.bfloat16),
        )

    normed_first, heads_major = lax.cond(section_at == 0, prepare, vacant, features)

    def allowed_block(start):
        local = lax.dynamic_slice_in_dim(places, start, block_rows)
        local_seg = lax.dynamic_slice_in_dim(segment, start, block_rows)
        return (local_seg[:, None] == segment[None, :]) & (
            usable[None, :] | (local[:, None] == places[None, :])
        )

    def attend_forward(incoming, micro_at):
        start = micro_at * block_rows
        allowed = allowed_block(start)
        queries = lax.dynamic_slice_in_dim(heads_major[0], start, block_rows, 1)

        def one_head(operands):
            query_head, key_head, value_head = operands
            scores = jnp.where(allowed, contract_last(query_head, key_head) * scale_big, MASKED)
            row_peak = jnp.max(scores, axis=-1, keepdims=True)
            lifted = jnp.exp(scores - row_peak)
            row_total = jnp.sum(lifted, axis=-1, keepdims=True)
            shares_low = (lifted / row_total).astype(jnp.bfloat16)
            mixed = jnp.dot(shares_low, value_head, preferred_element_type=jnp.float32)
            return (mixed.astype(jnp.bfloat16), (row_peak + jnp.log(row_total))[:, 0])

        mixed, logsum = lax.map(one_head, (queries, heads_major[1], heads_major[2]))
        attended = mixed.transpose(1, 0, 2).reshape(block_rows, model_width)
        residual = lax.dynamic_slice_in_dim(features, start, block_rows).astype(jnp.float32)
        finished = residual + jnp.dot(attended, attend_out, preferred_element_type=jnp.float32)
        return (finished.astype(jnp.bfloat16), attended, logsum)

    def mixer_forward(incoming, micro_at):
        widened = incoming.astype(jnp.float32)
        normed = normalize(widened, mixer_gain).astype(jnp.bfloat16)
        hidden = smooth(jnp.dot(normed, mixer_up, preferred_element_type=jnp.float32)).astype(
            jnp.bfloat16
        )
        finished = widened + jnp.dot(hidden, mixer_down, preferred_element_type=jnp.float32)
        return (finished.astype(jnp.bfloat16), incoming, zero_sums)

    def column_parts(incoming):
        widened = incoming.astype(jnp.float32).reshape(block_rows * attr_count, embed_width)
        normed = normalize(widened, column_gain).astype(jnp.bfloat16)
        projected = jnp.dot(normed, column_qkv, preferred_element_type=jnp.float32).astype(
            jnp.bfloat16
        )
        split_qkv = projected.reshape(block_rows, attr_count, 3, HEADS_ATTR, small_dim)
        queries = split_qkv[:, :, 0]
        keys_part = split_qkv[:, :, 1]
        values_part = split_qkv[:, :, 2]
        scores = (
            jnp.einsum("rahd,rbhd->rhab", queries, keys_part, preferred_element_type=jnp.float32)
            * scale_small
        )
        row_peak = jnp.max(scores, axis=-1, keepdims=True)
        lifted = jnp.exp(scores - row_peak)
        shares = lifted / jnp.sum(lifted, axis=-1, keepdims=True)
        shares_low = shares.astype(jnp.bfloat16)
        mixed = jnp.einsum(
            "rhab,rbhd->rahd", shares_low, values_part, preferred_element_type=jnp.float32
        )
        mixed = mixed.astype(jnp.bfloat16).reshape(block_rows * attr_count, embed_width)
        return (widened, normed, queries, keys_part, values_part, shares, shares_low, mixed)

    def column_forward(incoming, micro_at):
        parts = column_parts(incoming)
        finished = parts[0] + jnp.dot(parts[7], column_out, preferred_element_type=jnp.float32)
        return (finished.reshape(block_rows, model_width).astype(jnp.bfloat16), incoming, zero_sums)

    def column_mix_forward(incoming, micro_at):
        widened = incoming.astype(jnp.float32).reshape(block_rows * attr_count, embed_width)
        normed = normalize(widened, column_mix_gain).astype(jnp.bfloat16)
        hidden = smooth(jnp.dot(normed, column_up, preferred_element_type=jnp.float32)).astype(
            jnp.bfloat16
        )
        finished = widened + jnp.dot(hidden, column_down, preferred_element_type=jnp.float32)
        return (finished.reshape(block_rows, model_width).astype(jnp.bfloat16), incoming, zero_sums)

    forward_branches = (attend_forward, mixer_forward, column_forward, column_mix_forward)
    tick_count = MICRO + section_count - 1

    def forward_tick(tick_at, looped):
        incoming, kept, logsums, finished_all = looped
        micro_at = tick_at - section_at
        active = (micro_at >= 0) & (micro_at < MICRO)
        clipped = jnp.clip(micro_at, 0, MICRO - 1)

        def forward_run(block_in):
            return lax.switch(section_at, forward_branches, block_in, clipped)

        def forward_rest(block_in):
            return (jnp.zeros_like(block_in), jnp.zeros_like(block_in), zero_sums)

        finished, keep_block, logsum_block = lax.cond(active, forward_run, forward_rest, incoming)
        kept = lax.dynamic_update_index_in_dim(
            kept, jnp.where(active, keep_block, kept[clipped]), clipped, 0
        )
        logsums = lax.dynamic_update_index_in_dim(
            logsums, jnp.where(active, logsum_block, logsums[clipped]), clipped, 0
        )
        finished_all = lax.dynamic_update_index_in_dim(
            finished_all, jnp.where(active, finished, finished_all[clipped]), clipped, 0
        )
        sent = jax.tree.map(
            lambda part, own: part.astype(own.dtype),
            passed_along(shortened(finished), "section", -1),
            finished,
        )
        return (sent, kept, logsums, finished_all)

    start_forward = (
        jnp.zeros((block_rows, model_width), jnp.bfloat16),
        jnp.zeros((MICRO, block_rows, model_width), jnp.bfloat16),
        jnp.zeros((MICRO, head_count, block_rows), jnp.float32),
        jnp.zeros((MICRO, block_rows, model_width), jnp.bfloat16),
    )
    _, kept, logsums, finished_all = lax.fori_loop(0, tick_count, forward_tick, start_forward)

    def attend_backward(upstream, micro_at, kept_block, logsum_block, carried):
        gradients, query_acc, kv_acc = carried
        start = micro_at * block_rows
        allowed = allowed_block(start)
        out_grad = contract_rows(kept_block, upstream)
        pulled = contract_last(upstream, attend_out).astype(jnp.bfloat16)
        pulled_heads = pulled.reshape(block_rows, head_count, head_dim).transpose(1, 0, 2)
        queries = lax.dynamic_slice_in_dim(heads_major[0], start, block_rows, 1)

        def one_head(operands):
            query_head, key_head, value_head, pulled_head, logsum_head = operands
            scores = jnp.where(allowed, contract_last(query_head, key_head) * scale_big, MASKED)
            shares = jnp.exp(scores - logsum_head[:, None])
            shares_low = shares.astype(jnp.bfloat16)
            share_grad = contract_last(pulled_head, value_head)
            centre = jnp.sum(share_grad * shares, axis=-1, keepdims=True)
            score_grad = (shares * (share_grad - centre)).astype(jnp.bfloat16)
            query_grad = (
                jnp.dot(score_grad, key_head, preferred_element_type=jnp.float32) * scale_big
            )
            key_grad = contract_rows(score_grad, query_head) * scale_big
            value_grad = contract_rows(shares_low, pulled_head)
            return (query_grad, key_grad, value_grad)

        query_grad, key_grad, value_grad = lax.map(
            one_head, (queries, heads_major[1], heads_major[2], pulled_heads, logsum_block)
        )
        query_acc = lax.dynamic_update_slice_in_dim(query_acc, query_grad, start, 1)
        kv_acc = kv_acc + jnp.stack((key_grad, value_grad))
        gradients = add_at(gradients, 2, (out_grad,))
        return (upstream.astype(jnp.float32), (gradients, query_acc, kv_acc))

    def mixer_backward(upstream, micro_at, kept_block, logsum_block, carried):
        gradients, query_acc, kv_acc = carried
        widened = kept_block.astype(jnp.float32)
        input_part, gain_grad, up_grad, down_grad = mixer_back(
            widened, mixer_gain, mixer_up, mixer_down, upstream
        )
        gradients = add_at(gradients, 3, (gain_grad, up_grad, down_grad))
        return (input_part, (gradients, query_acc, kv_acc))

    def column_backward(upstream, micro_at, kept_block, logsum_block, carried):
        gradients, query_acc, kv_acc = carried
        widened, normed, queries, keys_part, values_part, shares, shares_low, mixed = column_parts(
            kept_block
        )
        flat_up = upstream.reshape(block_rows * attr_count, embed_width)
        out_grad = contract_rows(mixed, flat_up)
        pulled = contract_last(flat_up, column_out).astype(jnp.bfloat16)
        pulled = pulled.reshape(block_rows, attr_count, HEADS_ATTR, small_dim)
        share_grad = jnp.einsum(
            "rahd,rbhd->rhab", pulled, values_part, preferred_element_type=jnp.float32
        )
        centre = jnp.sum(share_grad * shares, axis=-1, keepdims=True)
        score_grad = (shares * (share_grad - centre)).astype(jnp.bfloat16)
        query_grad = (
            jnp.einsum("rhab,rbhd->rahd", score_grad, keys_part, preferred_element_type=jnp.float32)
            * scale_small
        )
        key_grad = (
            jnp.einsum("rhab,rahd->rbhd", score_grad, queries, preferred_element_type=jnp.float32)
            * scale_small
        )
        value_grad = jnp.einsum(
            "rhab,rahd->rbhd", shares_low, pulled, preferred_element_type=jnp.float32
        )
        projected_grad = jnp.stack((query_grad, key_grad, value_grad), axis=2).astype(jnp.bfloat16)
        projected_grad = projected_grad.reshape(block_rows * attr_count, 3 * embed_width)
        qkv_grad = contract_rows(normed, projected_grad)
        normed_grad = contract_last(projected_grad, column_qkv)
        widened_grad, gain_grad = normalize_back(widened, column_gain, normed_grad)
        input_part = (flat_up.astype(jnp.float32) + widened_grad).reshape(block_rows, model_width)
        gradients = add_at(gradients, 6, (gain_grad, qkv_grad, out_grad))
        return (input_part, (gradients, query_acc, kv_acc))

    def column_mix_backward(upstream, micro_at, kept_block, logsum_block, carried):
        gradients, query_acc, kv_acc = carried
        widened = kept_block.astype(jnp.float32).reshape(block_rows * attr_count, embed_width)
        flat_up = upstream.reshape(block_rows * attr_count, embed_width)
        input_part, gain_grad, up_grad, down_grad = mixer_back(
            widened, column_mix_gain, column_up, column_down, flat_up
        )
        gradients = add_at(gradients, 9, (gain_grad, up_grad, down_grad))
        return (input_part.reshape(block_rows, model_width), (gradients, query_acc, kv_acc))

    backward_branches = (attend_backward, mixer_backward, column_backward, column_mix_backward)
    weight_list = (
        attend_gain,
        attend_qkv,
        attend_out,
        mixer_gain,
        mixer_up,
        mixer_down,
        column_gain,
        column_qkv,
        column_out,
        column_mix_gain,
        column_up,
        column_down,
    )
    zero_grads = tuple((jnp.zeros(weight.shape, jnp.float32) for weight in weight_list))

    def backward_tick(tick_at, looped):
        incoming, carried, input_rows = looped
        micro_at = tick_at - (last_section - section_at)
        active = (micro_at >= 0) & (micro_at < MICRO)
        clipped = jnp.clip(micro_at, 0, MICRO - 1)
        final_rows = lax.dynamic_slice_in_dim(cotangent, clipped * block_rows, block_rows)
        upstream = jnp.where(section_at == last_section, final_rows, incoming)

        def backward_run(operands):
            return lax.switch(section_at, backward_branches, *operands)

        def backward_rest(operands):
            return (jnp.zeros((block_rows, model_width), jnp.float32), operands[4])

        grad_in, carried = lax.cond(
            active,
            backward_run,
            backward_rest,
            (upstream, clipped, kept[clipped], logsums[clipped], carried),
        )
        input_rows = lax.dynamic_update_index_in_dim(
            input_rows, jnp.where(active, grad_in, input_rows[clipped]), clipped, 0
        )
        sent = passed_along(grad_in.astype(jnp.bfloat16), "section", 1)
        return (sent, carried, input_rows)

    start_backward = (
        jnp.zeros((block_rows, model_width), jnp.bfloat16),
        (
            zero_grads,
            jnp.zeros((head_count, row_count, head_dim), jnp.float32),
            jnp.zeros((2, head_count, row_count, head_dim), jnp.float32),
        ),
        jnp.zeros((MICRO, block_rows, model_width), jnp.float32),
    )
    _, carried, input_rows = lax.fori_loop(0, tick_count, backward_tick, start_backward)
    gradients, query_acc, kv_acc = carried

    def finish_first(operands):
        grads_in, queries_acc, keys_acc, rows_in = operands
        heads_grad = jnp.concatenate((queries_acc[None], keys_acc), axis=0).astype(jnp.bfloat16)
        flat_grad = heads_grad.transpose(2, 0, 1, 3).reshape(row_count, 3 * model_width)
        qkv_grad = contract_rows(normed_first, flat_grad)
        normed_grad = contract_last(flat_grad, attend_qkv)
        widened_grad, gain_grad = normalize_back(
            features.astype(jnp.float32), attend_gain, normed_grad
        )
        grads_out = add_at(grads_in, 0, (gain_grad, qkv_grad))
        return (grads_out, rows_in.reshape(row_count, model_width) + widened_grad)

    def skip_first(operands):
        return (operands[0], operands[3].reshape(row_count, model_width))

    gradients, input_full = lax.cond(
        section_at == 0, finish_first, skip_first, (gradients, query_acc, kv_acc, input_rows)
    )
    quarter = model_width // section_count
    output_whole = finished_all.reshape(row_count, model_width)
    shared_out = broadcast(output_whole, "section", 0)
    result = lax.dynamic_slice_in_dim(shared_out, mesh_at * quarter, quarter, 1)
    shared_grad = broadcast(input_full.astype(jnp.bfloat16), "section", last_section).astype(
        input_full.dtype
    )
    input_grad = lax.dynamic_slice_in_dim(shared_grad, mesh_at * quarter, quarter, 1)
    row_parts = (
        lax.psum_scatter(gradients[0], ("dp", "section"), scatter_dimension=0, tiled=True),
        lax.psum_scatter(gradients[1], ("dp", "section"), scatter_dimension=0, tiled=True),
        lax.psum_scatter(gradients[2], ("dp", "section"), scatter_dimension=0, tiled=True),
        lax.psum_scatter(gradients[3], ("dp", "section"), scatter_dimension=0, tiled=True),
        lax.psum_scatter(gradients[4], ("dp", "section"), scatter_dimension=0, tiled=True),
        lax.psum_scatter(gradients[5], ("dp", "section"), scatter_dimension=0, tiled=True),
    )
    column_sums = lax.psum(
        (gradients[6], gradients[7], gradients[8], gradients[9], gradients[10], gradients[11]),
        ("dp", "section"),
    )
    return (
        result,
        input_grad,
        row_parts[0],
        row_parts[1],
        row_parts[2],
        row_parts[3],
        row_parts[4],
        row_parts[5],
        column_sums[0],
        column_sums[1],
        column_sums[2],
        column_sums[3],
        column_sums[4],
        column_sums[5],
    )


def solution(mesh):
    return jax.shard_map(
        body,
        mesh=mesh,
        in_specs=(
            P("dp", None),
            P("dp", None),
            P("dp", None),
            P("dp"),
            P(),
            P(),
            P(),
            P(),
            P(),
            P(),
            P(),
            P(),
            P(),
            P(),
            P(),
            P(),
        ),
        out_specs=(
            P("dp", "section"),
            P("dp", "section"),
            P(("dp", "section")),
            P(("dp", "section"), None),
            P(("dp", "section"), None),
            P(("dp", "section")),
            P(("dp", "section"), None),
            P(("dp", "section"), None),
            P(),
            P(),
            P(),
            P(),
            P(),
            P(),
        ),
        check_vma=False,
    )
```

profile of v0, /device:TPU:0, one launch (start us, length us, event | category | flops | bytes accessed | tf_op | source)
XLA Modules:
  0.0 3632.5 jit_solution(11489819380930049647)
XLA Ops:
  9.7 3.0 conditional.18
  16.9 602.0 %while.104 = (s32[]{:T(128)}, bf16[256,1024]{1,0:T(8,128)(2,1)}, bf16[4,256,1024]{1,2,0:T(8,128)(2,1)}, f32[4,8,256]{2,1,0:T(8,128)S(1)}, bf16[4,256,1024]{2,1,0...) while((s32[]{:T(128)}, bf16[256,1024]{1,0:T(8,128)(2,1)}, ...), condition=%wide.region_25.26_spmd.clone.clone, body=%wide.region_6.25_spmd.clone.clone.sunk | while | flops 4308600832 | bytes 43489224 | solution.py:250
  50.8 11.3 collective-permute-done.1
  72.1 9.5 collective-permute-done.1
  91.6 170.3 %collective-permute-done.1 = bf16[256,1024]{1,0:T(8,128)(2,1)} collective-permute-done((bf16[256,1024]{1,0:T(8,128)(2,1)}, bf16[256,1024]{1,0:T(8,128)(2,1)}, u32[]{:S(2)}, u32[]{:S(2)}) %collective-permute-start.1) | collective-permute-done | bytes 524320 | tf_op jit(solution)/shard_map/while/body/eval_jaxpr/ppermute | solution.py:24
  263.8 10.6 conditional.31
  263.8 10.6 conditional.4
  282.9 89.8 %collective-permute-done.1 = bf16[256,1024]{1,0:T(8,128)(2,1)} collective-permute-done((bf16[256,1024]{1,0:T(8,128)(2,1)}, bf16[256,1024]{1,0:T(8,128)(2,1)}, u32[]{:S(2)}, u32[]{:S(2)}) %collective-permute-start.1) | collective-permute-done | bytes 524320 | tf_op jit(solution)/shard_map/while/body/eval_jaxpr/ppermute | solution.py:24
  374.6 10.6 conditional.31
  374.6 10.6 conditional.4
  393.8 88.9 %collective-permute-done.1 = bf16[256,1024]{1,0:T(8,128)(2,1)} collective-permute-done((bf16[256,1024]{1,0:T(8,128)(2,1)}, bf16[256,1024]{1,0:T(8,128)(2,1)}, u32[]{:S(2)}, u32[]{:S(2)}) %collective-permute-start.1) | collective-permute-done | bytes 524320 | tf_op jit(solution)/shard_map/while/body/eval_jaxpr/ppermute | solution.py:24
  484.6 10.6 conditional.31
  484.6 10.6 conditional.4
  503.7 88.0 %collective-permute-done.1 = bf16[256,1024]{1,0:T(8,128)(2,1)} collective-permute-done((bf16[256,1024]{1,0:T(8,128)(2,1)}, bf16[256,1024]{1,0:T(8,128)(2,1)}, u32[]{:S(2)}, u32[]{:S(2)}) %collective-permute-start.1) | collective-permute-done | bytes 524320 | tf_op jit(solution)/shard_map/while/body/eval_jaxpr/ppermute | solution.py:24
  593.6 10.6 conditional.31
  593.6 10.6 conditional.4
  622.1 7.8 broadcast_in_dim.178
  629.9 7.9 broadcast_in_dim.179
  643.0 4.1 broadcast_in_dim.184
  649.6 1354.1 %while.105 = (s32[]{:T(128)}, bf16[256,1024]{1,0:T(8,128)(2,1)S(1)}, f32[1024,1024]{1,0:T(8,128)}, f32[1024]{0:T(1024)}, f32[1024,4096]{1,0:T(8,128)}, /*index=5...) while((s32[]{:T(128)}, bf16[256,1024]{1,0:T(8,128)(2,1)S(1)}, ...), condition=%wide.region_55.56_spmd.clone.clone, body=%wide.region_27.55_spmd.clone.clone.sunk | while | flops 10792208384 | bytes 162951520 | solution.py:389
  650.5 58.8 %conditional.32 = ((f32[256,1024]{1,0:T(8,128)}, f32[1024,1024]{1,0:T(8,128)}, f32[1024]{0:T(1024)}, f32[1024,4096]{1,0:T(8,128)}, f32[4096,1024]{1,0:T(8,128)},...) conditional(s32[]{:T(128)} %convert_element_type.423, ...), branch_computations={%region_28.28_spmd, %region_29.54_spmd} | conditional | flops 10791684096 | bytes 153729920 | solution.py:368
  653.1 54.8 %conditional.6 = (f32[256,1024]{1,0:T(8,128)}, f32[1024,1024]{1,0:T(8,128)}, f32[1024]{0:T(1024)}, f32[1024,4096]{1,0:T(8,128)}, f32[4096,1024]{1,0:T(8,128)}, /...) conditional(s32[]{:T(128)} %clamp.7, ...), branch_computations={%region_30.32_spmd, %region_34.38_spmd, %region_40.47_spmd, %regio... | conditional | flops 10791421952 | bytes 150059232 | solution.py:363
  689.6 3.9 fusion.137
  696.2 3.2 copy.245
  702.8 4.0 fusion.141
  719.7 58.6 %conditional.32 = ((f32[256,1024]{1,0:T(8,128)}, f32[1024,1024]{1,0:T(8,128)}, f32[1024]{0:T(1024)}, f32[1024,4096]{1,0:T(8,128)}, f32[4096,1024]{1,0:T(8,128)},...) conditional(s32[]{:T(128)} %convert_element_type.423, ...), branch_computations={%region_28.28_spmd, %region_29.54_spmd} | conditional | flops 10791684096 | bytes 153729920 | solution.py:368
  722.3 54.7 %conditional.6 = (f32[256,1024]{1,0:T(8,128)}, f32[1024,1024]{1,0:T(8,128)}, f32[1024]{0:T(1024)}, f32[1024,4096]{1,0:T(8,128)}, f32[4096,1024]{1,0:T(8,128)}, /...) conditional(s32[]{:T(128)} %clamp.7, ...), branch_computations={%region_30.32_spmd, %region_34.38_spmd, %region_40.47_spmd, %regio... | conditional | flops 10791421952 | bytes 150059232 | solution.py:363
  758.8 3.9 fusion.137
  765.4 3.2 copy.245
  772.0 4.0 fusion.141
  779.7 223.7 %collective-permute-start = (bf16[256,1024]{1,0:T(8,128)(2,1)S(1)}, bf16[256,1024]{1,0:T(8,128)(2,1)S(1)}, u32[]{:S(2)}, u32[]{:S(2)}) collective-permute-start(bf16[256,1024]{1,0:T(8,128)(2,1)S(1)} %convert_element_type.424), channel_id=1, source_target_pairs={{0,1},{1,2},{2,3},{4,5},{5,6},{6,7},{8,9},{9,10},{10,11},{12,13},{... | collective-permute-start | bytes 1572872 | tf_op jit(solution)/shard_map/while/body/eval_jaxpr/ppermute | solution.py:24
  1007.1 3.0 collective-permute-done
  1011.0 59.1 %conditional.32 = ((f32[256,1024]{1,0:T(8,128)}, f32[1024,1024]{1,0:T(8,128)}, f32[1024]{0:T(1024)}, f32[1024,4096]{1,0:T(8,128)}, f32[4096,1024]{1,0:T(8,128)},...) conditional(s32[]{:T(128)} %convert_element_type.423, ...), branch_computations={%region_28.28_spmd, %region_29.54_spmd} | conditional | flops 10791684096 | bytes 153729920 | solution.py:368
  1013.6 54.9 %conditional.6 = (f32[256,1024]{1,0:T(8,128)}, f32[1024,1024]{1,0:T(8,128)}, f32[1024]{0:T(1024)}, f32[1024,4096]{1,0:T(8,128)}, f32[4096,1024]{1,0:T(8,128)}, /...) conditional(s32[]{:T(128)} %clamp.7, ...), branch_computations={%region_30.32_spmd, %region_34.38_spmd, %region_40.47_spmd, %regio... | conditional | flops 10791421952 | bytes 150059232 | solution.py:363
  1050.2 3.9 fusion.137
  1056.8 3.2 copy.245
  1063.4 4.0 fusion.141
  1071.4 228.7 %collective-permute-start = (bf16[256,1024]{1,0:T(8,128)(2,1)S(1)}, bf16[256,1024]{1,0:T(8,128)(2,1)S(1)}, u32[]{:S(2)}, u32[]{:S(2)}) collective-permute-start(bf16[256,1024]{1,0:T(8,128)(2,1)S(1)} %convert_element_type.424), channel_id=1, source_target_pairs={{0,1},{1,2},{2,3},{4,5},{5,6},{6,7},{8,9},{9,10},{10,11},{12,13},{... | collective-permute-start | bytes 1572872 | tf_op jit(solution)/shard_map/while/body/eval_jaxpr/ppermute | solution.py:24
  1303.8 3.0 collective-permute-done
  1307.6 58.7 %conditional.32 = ((f32[256,1024]{1,0:T(8,128)}, f32[1024,1024]{1,0:T(8,128)}, f32[1024]{0:T(1024)}, f32[1024,4096]{1,0:T(8,128)}, f32[4096,1024]{1,0:T(8,128)},...) conditional(s32[]{:T(128)} %convert_element_type.423, ...), branch_computations={%region_28.28_spmd, %region_29.54_spmd} | conditional | flops 10791684096 | bytes 153729920 | solution.py:368
  1310.2 54.8 %conditional.6 = (f32[256,1024]{1,0:T(8,128)}, f32[1024,1024]{1,0:T(8,128)}, f32[1024]{0:T(1024)}, f32[1024,4096]{1,0:T(8,128)}, f32[4096,1024]{1,0:T(8,128)}, /...) conditional(s32[]{:T(128)} %clamp.7, ...), branch_computations={%region_30.32_spmd, %region_34.38_spmd, %region_40.47_spmd, %regio... | conditional | flops 10791421952 | bytes 150059232 | solution.py:363
  1346.7 3.9 fusion.137
  1353.3 3.2 copy.245
  1359.9 4.0 fusion.141
  1367.7 229.5 %collective-permute-start = (bf16[256,1024]{1,0:T(8,128)(2,1)S(1)}, bf16[256,1024]{1,0:T(8,128)(2,1)S(1)}, u32[]{:S(2)}, u32[]{:S(2)}) collective-permute-start(bf16[256,1024]{1,0:T(8,128)(2,1)S(1)} %convert_element_type.424), channel_id=1, source_target_pairs={{0,1},{1,2},{2,3},{4,5},{5,6},{6,7},{8,9},{9,10},{10,11},{12,13},{... | collective-permute-start | bytes 1572872 | tf_op jit(solution)/shard_map/while/body/eval_jaxpr/ppermute | solution.py:24
  1605.0 9.0 conditional.32
  1615.3 278.3 %collective-permute-start = (bf16[256,1024]{1,0:T(8,128)(2,1)S(1)}, bf16[256,1024]{1,0:T(8,128)(2,1)S(1)}, u32[]{:S(2)}, u32[]{:S(2)}) collective-permute-start(bf16[256,1024]{1,0:T(8,128)(2,1)S(1)} %convert_element_type.424), channel_id=1, source_target_pairs={{0,1},{1,2},{2,3},{4,5},{5,6},{6,7},{8,9},{9,10},{10,11},{12,13},{... | collective-permute-start | bytes 1572872 | tf_op jit(solution)/shard_map/while/body/eval_jaxpr/ppermute | solution.py:24
  1896.1 4.2 collective-permute-done
  1903.5 12.7 collective-permute-start
  1918.8 4.2 collective-permute-done
  1926.0 62.4 %collective-permute-start = (bf16[256,1024]{1,0:T(8,128)(2,1)S(1)}, bf16[256,1024]{1,0:T(8,128)(2,1)S(1)}, u32[]{:S(2)}, u32[]{:S(2)}) collective-permute-start(bf16[256,1024]{1,0:T(8,128)(2,1)S(1)} %convert_element_type.424), channel_id=1, source_target_pairs={{0,1},{1,2},{2,3},{4,5},{5,6},{6,7},{8,9},{9,10},{10,11},{12,13},{... | collective-permute-start | bytes 1572872 | tf_op jit(solution)/shard_map/while/body/eval_jaxpr/ppermute | solution.py:24
  1990.9 4.2 collective-permute-done
  2003.7 9.9 conditional.19
  2003.7 3.8 convert_element_type.248
  2007.5 6.1 broadcast_in_dim.142
  2014.3 3.1 broadcast_select_fusion.1
  2020.2 12.6 copy.263
  2034.2 252.4 %all-reduce.9.cloned.1.call-done = (f32[1024]{0:T(1024)}, f32[1024]{0:T(1024)}, f32[64]{0:T(128)}, f32[64,192]{1,0:T(8,128)}, f32[64,64]{1,0:T(8,128)}, /*index=5*/f32[64]{0:T(128)}) async-done(((f32[1024]{0:T(1024)}, f32[1024]{0:T(1024)}, f32[64]{0:T(128)}, f32[64,192]{1,0:T(8,128)}, f32[64,64]{1,0:T(8,128)}, /*index=5*/f32[64]{0:T(128)}), (f32[1024]{0:T(1024)}, f32[1024]{0:T(1024)}, f32[64]{0:T(128)}, ...) | async-done | bytes 74256
  2289.1 156.3 %all-reduce.13.cloned.1.call-done = (bf16[1024,1024]{1,0:T(8,128)(2,1)}, bf16[1024,1024]{1,0:T(8,128)(2,1)}) async-done(((bf16[1024,1024]{1,0:T(8,128)(2,1)}, bf16[1024,1024]{1,0:T(8,128)(2,1)}), (bf16[1024,1024]{1,0:T(8,128)(2,1)}, bf16[1024,1024]{1,0:T(8,128)(2,1)})) %all-reduce.13.cloned.1.call-update) | async-done | bytes 4194320 | tf_op jit(solution)/shard_map/psum | solution.py:29
  2447.9 126.6 %all-reduce.11.cloned.1.call-done = (f32[64,256]{1,0:T(8,128)}, f32[256,64]{0,1:T(8,128)}) async-done(((f32[64,256]{1,0:T(8,128)}, f32[256,64]{0,1:T(8,128)}), (f32[64,256]{1,0:T(8,128)}, f32[256,64]{0,1:T(8,128)})) %all-reduce.11.cloned.1.call-update) | async-done | bytes 131088 | tf_op jit(solution)/shard_map/psum | solution.py:426
  2574.5 150.4 %reduce-scatter.7.cloned.1.call-done = f32[32,1024]{1,0:T(8,128)} async-done(((f32[1024,1024]{1,0:T(8,128)}), f32[32,1024]{1,0:T(8,128)}) %reduce-scatter.7.cloned.1.call-update) | async-done | bytes 131088 | tf_op jit(solution)/shard_map/reduce_scatter | solution.py:421
  2724.8 161.2 %reduce-scatter.5.cloned.1.call-done = f32[32,3072]{1,0:T(8,128)} async-done(((f32[1024,3072]{1,0:T(8,128)}), f32[32,3072]{1,0:T(8,128)}) %reduce-scatter.5.cloned.1.call-update) | async-done | bytes 393232 | tf_op jit(solution)/shard_map/reduce_scatter | solution.py:420
  2886.0 366.1 %reduce-scatter.9.cloned.1.call-done = f32[32,4096]{1,0:T(8,128)} async-done(((f32[1024,4096]{1,0:T(8,128)}), f32[32,4096]{1,0:T(8,128)}) %reduce-scatter.9.cloned.1.call-update) | async-done | bytes 524304 | tf_op jit(solution)/shard_map/reduce_scatter | solution.py:423
  3252.1 365.1 %reduce-scatter.11.cloned.1.call-done = f32[128,1024]{1,0:T(8,128)} async-done(((f32[4096,1024]{1,0:T(8,128)}), f32[128,1024]{1,0:T(8,128)}) %reduce-scatter.11.cloned.1.call-update) | async-done | bytes 524304 | tf_op jit(solution)/shard_map/reduce_scatter | solution.py:424
  (510 shorter events, 278.4 us)
Async XLA Ops:
  7.2 2279.4 %all-reduce.9.cloned.1.call-start = ((), (), s32[]{:S(2)}) async-start(), calls=%async_computation.8 | async-start | bytes 215040
  45.0 17.2 collective-permute-start.1
  66.3 15.3 collective-permute-start.1
  85.8 176.1 %collective-permute-start.1 = (bf16[256,1024]{1,0:T(8,128)(2,1)}, bf16[256,1024]{1,0:T(8,128)(2,1)}, u32[]{:S(2)}, u32[]{:S(2)}) collective-permute-start(bf16[256,1024]{1,0:T(8,128)(2,1)} %get-tuple-element.3483), channel_id=1, source_target_pairs={{1,0},{2,1},{3,2},{5,4},{6,5},{7,6},{9,8},{10,9},{11,10},{13,12},{... | collective-permute-start | bytes 1572872 | tf_op jit(solution)/shard_map/while/body/eval_jaxpr/ppermute | solution.py:24
  274.3 98.4 %collective-permute-start.1 = (bf16[256,1024]{1,0:T(8,128)(2,1)}, bf16[256,1024]{1,0:T(8,128)(2,1)}, u32[]{:S(2)}, u32[]{:S(2)}) collective-permute-start(bf16[256,1024]{1,0:T(8,128)(2,1)} %get-tuple-element.3483), channel_id=1, source_target_pairs={{1,0},{2,1},{3,2},{5,4},{6,5},{7,6},{9,8},{10,9},{11,10},{13,12},{... | collective-permute-start | bytes 1572872 | tf_op jit(solution)/shard_map/while/body/eval_jaxpr/ppermute | solution.py:24
  385.2 97.5 %collective-permute-start.1 = (bf16[256,1024]{1,0:T(8,128)(2,1)}, bf16[256,1024]{1,0:T(8,128)(2,1)}, u32[]{:S(2)}, u32[]{:S(2)}) collective-permute-start(bf16[256,1024]{1,0:T(8,128)(2,1)} %get-tuple-element.3483), channel_id=1, source_target_pairs={{1,0},{2,1},{3,2},{5,4},{6,5},{7,6},{9,8},{10,9},{11,10},{13,12},{... | collective-permute-start | bytes 1572872 | tf_op jit(solution)/shard_map/while/body/eval_jaxpr/ppermute | solution.py:24
  495.1 96.6 %collective-permute-start.1 = (bf16[256,1024]{1,0:T(8,128)(2,1)}, bf16[256,1024]{1,0:T(8,128)(2,1)}, u32[]{:S(2)}, u32[]{:S(2)}) collective-permute-start(bf16[256,1024]{1,0:T(8,128)(2,1)} %get-tuple-element.3483), channel_id=1, source_target_pairs={{1,0},{2,1},{3,2},{5,4},{6,5},{7,6},{9,8},{10,9},{11,10},{13,12},{... | collective-permute-start | bytes 1572872 | tf_op jit(solution)/shard_map/while/body/eval_jaxpr/ppermute | solution.py:24
  604.2 11.4 collective-permute-start.1
  618.9 11.0 copy-start.39
  649.6 1354.1 %copy-start.44 = (f32[1024]{0:T(1024)S(1)}, f32[1024]{0:T(1024)}, u32[]{:S(2)}) copy-start(f32[1024]{0:T(1024)} %param.44) | copy-start | bytes 12292
  683.5 5.0 copy-start.21
  683.5 5.0 copy-start.35
  694.9 7.3 copy-start.52
  694.9 7.3 copy-start.24
  696.2 6.5 copy-start.17
  709.2 9.3 copy-start.33
  709.3 9.3 copy-start.42
  709.3 9.3 copy-start.48
  710.6 8.0 collective-permute-start
  752.7 5.0 copy-start.21
  752.7 5.0 copy-start.35
  764.1 7.3 copy-start.52
  764.1 7.3 copy-start.24
  765.4 6.5 copy-start.17
  778.3 231.7 %copy-start.33 = (f32[4,8,256]{2,1,0:T(8,128)S(1)}, f32[4,8,256]{2,1,0:T(8,128)}, u32[]{:S(2)}) copy-start(f32[4,8,256]{2,1,0:T(8,128)} %copy-done.32) | copy-start | bytes 98308 | tf_op jit(solution)/shard_map/while
  778.4 231.7 %copy-start.42 = (s32[1024]{0:T(1024)S(1)}, s32[1024]{0:T(1024)}, u32[]{:S(2)}) copy-start(s32[1024]{0:T(1024)} %copy-done.41) | copy-start | bytes 12292 | tf_op jit(solution)/shard_map/while
  778.4 231.7 %copy-start.48 = (pred[1024]{0:T(1024)(128)(4,1)S(1)}, pred[1024]{0:T(1024)(128)(4,1)}, u32[]{:S(2)}) copy-start(pred[1024]{0:T(1024)(128)(4,1)} %copy-done.47) | copy-start | bytes 3076 | tf_op jit(solution)/shard_map/while
  779.7 230.4 %collective-permute-start = (bf16[256,1024]{1,0:T(8,128)(2,1)S(1)}, bf16[256,1024]{1,0:T(8,128)(2,1)S(1)}, u32[]{:S(2)}, u32[]{:S(2)}) collective-permute-start(bf16[256,1024]{1,0:T(8,128)(2,1)S(1)} %convert_element_type.424), channel_id=1, source_target_pairs={{0,1},{1,2},{2,3},{4,5},{5,6},{6,7},{8,9},{9,10},{10,11},{12,13},{... | collective-permute-start | bytes 1572872 | tf_op jit(solution)/shard_map/while/body/eval_jaxpr/ppermute | solution.py:24
  1044.1 5.0 copy-start.21
  1044.1 5.0 copy-start.35
  1055.4 7.3 copy-start.52
  1055.5 7.3 copy-start.24
  1056.8 6.5 copy-start.17
  1070.1 236.7 %copy-start.33 = (f32[4,8,256]{2,1,0:T(8,128)S(1)}, f32[4,8,256]{2,1,0:T(8,128)}, u32[]{:S(2)}) copy-start(f32[4,8,256]{2,1,0:T(8,128)} %copy-done.32) | copy-start | bytes 98308 | tf_op jit(solution)/shard_map/while
  1070.1 236.7 %copy-start.42 = (s32[1024]{0:T(1024)S(1)}, s32[1024]{0:T(1024)}, u32[]{:S(2)}) copy-start(s32[1024]{0:T(1024)} %copy-done.41) | copy-start | bytes 12292 | tf_op jit(solution)/shard_map/while
  1070.1 236.7 %copy-start.48 = (pred[1024]{0:T(1024)(128)(4,1)S(1)}, pred[1024]{0:T(1024)(128)(4,1)}, u32[]{:S(2)}) copy-start(pred[1024]{0:T(1024)(128)(4,1)} %copy-done.47) | copy-start | bytes 3076 | tf_op jit(solution)/shard_map/while
  1071.4 235.4 %collective-permute-start = (bf16[256,1024]{1,0:T(8,128)(2,1)S(1)}, bf16[256,1024]{1,0:T(8,128)(2,1)S(1)}, u32[]{:S(2)}, u32[]{:S(2)}) collective-permute-start(bf16[256,1024]{1,0:T(8,128)(2,1)S(1)} %convert_element_type.424), channel_id=1, source_target_pairs={{0,1},{1,2},{2,3},{4,5},{5,6},{6,7},{8,9},{9,10},{10,11},{12,13},{... | collective-permute-start | bytes 1572872 | tf_op jit(solution)/shard_map/while/body/eval_jaxpr/ppermute | solution.py:24
  1340.6 5.0 copy-start.21
  1340.6 5.0 copy-start.35
  1352.0 7.3 copy-start.52
  1352.0 7.3 copy-start.24
  1353.3 6.5 copy-start.17
  1366.3 237.5 %copy-start.33 = (f32[4,8,256]{2,1,0:T(8,128)S(1)}, f32[4,8,256]{2,1,0:T(8,128)}, u32[]{:S(2)}) copy-start(f32[4,8,256]{2,1,0:T(8,128)} %copy-done.32) | copy-start | bytes 98308 | tf_op jit(solution)/shard_map/while
  1366.3 237.5 %copy-start.42 = (s32[1024]{0:T(1024)S(1)}, s32[1024]{0:T(1024)}, u32[]{:S(2)}) copy-start(s32[1024]{0:T(1024)} %copy-done.41) | copy-start | bytes 12292 | tf_op jit(solution)/shard_map/while
  1366.3 237.5 %copy-start.48 = (pred[1024]{0:T(1024)(128)(4,1)S(1)}, pred[1024]{0:T(1024)(128)(4,1)}, u32[]{:S(2)}) copy-start(pred[1024]{0:T(1024)(128)(4,1)} %copy-done.47) | copy-start | bytes 3076 | tf_op jit(solution)/shard_map/while
  1367.7 236.2 %collective-permute-start = (bf16[256,1024]{1,0:T(8,128)(2,1)S(1)}, bf16[256,1024]{1,0:T(8,128)(2,1)S(1)}, u32[]{:S(2)}, u32[]{:S(2)}) collective-permute-start(bf16[256,1024]{1,0:T(8,128)(2,1)S(1)} %convert_element_type.424), channel_id=1, source_target_pairs={{0,1},{1,2},{2,3},{4,5},{5,6},{6,7},{8,9},{9,10},{10,11},{12,13},{... | collective-permute-start | bytes 1572872 | tf_op jit(solution)/shard_map/while/body/eval_jaxpr/ppermute | solution.py:24
  1614.0 286.3 %copy-start.33 = (f32[4,8,256]{2,1,0:T(8,128)S(1)}, f32[4,8,256]{2,1,0:T(8,128)}, u32[]{:S(2)}) copy-start(f32[4,8,256]{2,1,0:T(8,128)} %copy-done.32) | copy-start | bytes 98308 | tf_op jit(solution)/shard_map/while
  1614.0 286.3 %copy-start.42 = (s32[1024]{0:T(1024)S(1)}, s32[1024]{0:T(1024)}, u32[]{:S(2)}) copy-start(s32[1024]{0:T(1024)} %copy-done.41) | copy-start | bytes 12292 | tf_op jit(solution)/shard_map/while
  1614.0 286.3 %copy-start.48 = (pred[1024]{0:T(1024)(128)(4,1)S(1)}, pred[1024]{0:T(1024)(128)(4,1)}, u32[]{:S(2)}) copy-start(pred[1024]{0:T(1024)(128)(4,1)} %copy-done.47) | copy-start | bytes 3076 | tf_op jit(solution)/shard_map/while
  1615.3 284.9 %collective-permute-start = (bf16[256,1024]{1,0:T(8,128)(2,1)S(1)}, bf16[256,1024]{1,0:T(8,128)(2,1)S(1)}, u32[]{:S(2)}, u32[]{:S(2)}) collective-permute-start(bf16[256,1024]{1,0:T(8,128)(2,1)S(1)} %convert_element_type.424), channel_id=1, source_target_pairs={{0,1},{1,2},{2,3},{4,5},{5,6},{6,7},{8,9},{9,10},{10,11},{12,13},{... | collective-permute-start | bytes 1572872 | tf_op jit(solution)/shard_map/while/body/eval_jaxpr/ppermute | solution.py:24
  1902.2 20.7 copy-start.33
  1902.2 20.7 copy-start.42
  1902.2 20.7 copy-start.48
  1903.5 19.4 collective-permute-start
  1924.7 70.4 %copy-start.33 = (f32[4,8,256]{2,1,0:T(8,128)S(1)}, f32[4,8,256]{2,1,0:T(8,128)}, u32[]{:S(2)}) copy-start(f32[4,8,256]{2,1,0:T(8,128)} %copy-done.32) | copy-start | bytes 98308 | tf_op jit(solution)/shard_map/while
  1924.7 70.4 %copy-start.42 = (s32[1024]{0:T(1024)S(1)}, s32[1024]{0:T(1024)}, u32[]{:S(2)}) copy-start(s32[1024]{0:T(1024)} %copy-done.41) | copy-start | bytes 12292 | tf_op jit(solution)/shard_map/while
  1924.7 70.4 %copy-start.48 = (pred[1024]{0:T(1024)(128)(4,1)S(1)}, pred[1024]{0:T(1024)(128)(4,1)}, u32[]{:S(2)}) copy-start(pred[1024]{0:T(1024)(128)(4,1)} %copy-done.47) | copy-start | bytes 3076 | tf_op jit(solution)/shard_map/while
  1926.0 69.1 %collective-permute-start = (bf16[256,1024]{1,0:T(8,128)(2,1)S(1)}, bf16[256,1024]{1,0:T(8,128)(2,1)S(1)}, u32[]{:S(2)}, u32[]{:S(2)}) collective-permute-start(bf16[256,1024]{1,0:T(8,128)(2,1)S(1)} %convert_element_type.424), channel_id=1, source_target_pairs={{0,1},{1,2},{2,3},{4,5},{5,6},{6,7},{8,9},{9,10},{10,11},{12,13},{... | collective-permute-start | bytes 1572872 | tf_op jit(solution)/shard_map/while/body/eval_jaxpr/ppermute | solution.py:24
  2014.2 431.2 %all-reduce.13.cloned.1.call-start = ((), (), s32[]{:S(2)}) async-start(), calls=%async_computation.10 | async-start | bytes 8388608 | tf_op jit(solution)/shard_map/psum | solution.py:29
  2018.8 555.7 %all-reduce.11.cloned.1.call-start = ((), (), s32[]{:S(2)}) async-start(), calls=%async_computation.9 | async-start | bytes 262144 | tf_op jit(solution)/shard_map/psum | solution.py:426
  2019.6 705.2 %reduce-scatter.7.cloned.1.call-start = ((), (), s32[]{:S(2)}) async-start(), calls=%async_computation.5 | async-start | bytes 4325376 | tf_op jit(solution)/shard_map/reduce_scatter | solution.py:421
  2020.2 865.8 %reduce-scatter.5.cloned.1.call-start = ((), (), s32[]{:S(2)}) async-start(), calls=%async_computation.4 | async-start | bytes 12976128 | tf_op jit(solution)/shard_map/reduce_scatter | solution.py:420
  2032.8 1219.2 %reduce-scatter.9.cloned.1.call-start = ((), (), s32[]{:S(2)}) async-start(), calls=%async_computation.6 | async-start | bytes 17301504 | tf_op jit(solution)/shard_map/reduce_scatter | solution.py:423
  2033.4 1583.7 %reduce-scatter.11.cloned.1.call-start = ((), (), s32[]{:S(2)}) async-start(), calls=%async_computation.7 | async-start | bytes 17301504 | tf_op jit(solution)/shard_map/reduce_scatter | solution.py:424
  (58 other events, 110.7 us)
Sparse Core Ops, SparseCore 0:
  2014.3 272.2 all-reduce.8
  2289.0 156.3 all-reduce.12
  2452.7 121.7 all-reduce.10
  2577.3 147.5 reduce-scatter.6
  2732.3 153.6 reduce-scatter.4
  2888.7 363.2 reduce-scatter.8
  3254.9 362.1 reduce-scatter.10
where the time goes:
time: 3650 us; the launch traced here: 3630 us
  waiting for transfers between devices  2060 us (56%)
  starting transfers between devices  1050 us (29%)
  local copies, waits for them, and re-layouts  210 us (6%)
  loops' own time  169 us (5%)
  other arithmetic  76.4 us (2%)
  matrix products  51.3 us (1%)
    ppermute x14, starting transfers between devices, passed_along(): lax.ppermute(value, axis, [(source, source + steps) for source in range(l...  1050 us
    ppermute x14, waiting for transfers between devices, passed_along(): lax.ppermute(value, axis, [(source, source + steps) for source in range(l...  485 us
    reduce_scatter x1, waiting for transfers between devices, body(): lax.psum_scatter(gradients[4], ('dp', 'section'), scatter_dimension=0, ti...  366 us
    reduce_scatter x1, waiting for transfers between devices, body(): lax.psum_scatter(gradients[5], ('dp', 'section'), scatter_dimension=0, ti...  365 us
    unnamed x8, waiting for transfers between devices  254 us
    reduce_scatter x1, waiting for transfers between devices, body(): lax.psum_scatter(gradients[1], ('dp', 'section'), scatter_dimension=0, ti...  161 us
    psum x1, waiting for transfers between devices, broadcast(): return lax.psum(kept, axis)  156 us
    reduce_scatter x1, waiting for transfers between devices, body(): lax.psum_scatter(gradients[2], ('dp', 'section'), scatter_dimension=0, ti...  150 us
  transfers between devices with their start and end apart: 21, of which 21 were waited for; matrix products, arithmetic and copies ran while one was open for 2% of the time, Pallas kernels for 0%

commit v1 on v0

v1 whole, which is shorter than its diff:
```python
import functools

import jax
import jax.numpy as jnp
from jax import lax
from jax.experimental import pallas as pl
from jax.experimental.pallas import tpu as pltpu
from jax.sharding import PartitionSpec as P

ATTR = 16
HEADS = 8
HEADS_ATTR = 8

EPSILON = 1e-05
MASKED = -1e30
GELU_SCALE = 0.7978845608028654
GELU_CUBE = 0.044715
BF16 = jnp.bfloat16
F32 = jnp.float32


def exchanged(value, axis, mask):
    count = lax.axis_size(axis)
    return lax.ppermute(value, axis, [(at, at ^ mask) for at in range(count)])


def normal_parts(vector, axis=-1):
    centred = vector - jnp.mean(vector, axis=axis, keepdims=True)
    rate = lax.rsqrt(jnp.mean(centred * centred, axis=axis, keepdims=True) + EPSILON)
    return centred * rate, rate


def normal_back(normed, rate, scaled, axis=-1):
    middle = jnp.mean(scaled, axis=axis, keepdims=True)
    along = jnp.mean(scaled * normed, axis=axis, keepdims=True)
    return rate * (scaled - middle - normed * along)


def smooth(inputs):
    inner = GELU_SCALE * (inputs + GELU_CUBE * inputs * inputs * inputs)
    return 0.5 * inputs * (1.0 + jnp.tanh(inner))


def smooth_pair(inputs):
    square = inputs * inputs
    bent = jnp.tanh(GELU_SCALE * inputs * (1.0 + GELU_CUBE * square))
    half = 0.5 * (1.0 + bent)
    slope = half + (0.5 * GELU_SCALE) * inputs * (1.0 - bent * bent) * (
        1.0 + (3.0 * GELU_CUBE) * square
    )
    return inputs * half, slope


def dot(left, right):
    return jnp.dot(left, right, preferred_element_type=F32)


def dot_rows(left, right):
    return lax.dot_general(left, right, (((0,), (0,)), ((), ())), preferred_element_type=F32)


def dot_last(left, right):
    return lax.dot_general(left, right, (((1,), (1,)), ((), ())), preferred_element_type=F32)


def attend_forward_kernel(q_ref, k_ref, v_ref, mask_ref, out_ref, *, scale):
    scores = jnp.where(mask_ref[...] > 0, dot_last(q_ref[...], k_ref[...]) * scale, MASKED)
    lifted = jnp.exp(scores - jnp.max(scores, axis=-1, keepdims=True))
    shares = (lifted / jnp.sum(lifted, axis=-1, keepdims=True)).astype(BF16)
    out_ref[...] = dot(shares, v_ref[...]).astype(BF16)


def attend_forward(projected, mask, own_rows):
    rows, wide = projected.shape
    width = wide // 3
    head_dim = width // HEADS
    return pl.pallas_call(
        functools.partial(attend_forward_kernel, scale=head_dim**-0.5),
        grid=(HEADS,),
        in_specs=[
            pl.BlockSpec((own_rows, head_dim), lambda h: (0, h)),
            pl.BlockSpec((rows, head_dim), lambda h: (0, HEADS + h)),
            pl.BlockSpec((rows, head_dim), lambda h: (0, 2 * HEADS + h)),
            pl.BlockSpec((own_rows, rows), lambda h: (0, 0)),
        ],
        out_specs=pl.BlockSpec((own_rows, head_dim), lambda h: (0, h)),
        out_shape=jax.ShapeDtypeStruct((own_rows, width), BF16),
        compiler_params=pltpu.CompilerParams(vmem_limit_bytes=48 * 2**20),
        name="attend_forward",
    )(projected, projected, projected, mask)


def attend_backward_kernel(
    first_ref, q_ref, k_ref, v_ref, up_ref, mask_ref, mixed_ref, dq_ref, dk_ref, dv_ref, *, scale
):
    queries, keys, values, upstream = q_ref[...], k_ref[...], v_ref[...], up_ref[...]
    scores = jnp.where(mask_ref[...] > 0, dot_last(queries, keys) * scale, MASKED)
    lifted = jnp.exp(scores - jnp.max(scores, axis=-1, keepdims=True))
    shares = lifted / jnp.sum(lifted, axis=-1, keepdims=True)
    shares_low = shares.astype(BF16)
    mixed_ref[...] = dot(shares_low, values).astype(BF16)
    share_grad = dot_last(upstream, values)
    centre = jnp.sum(share_grad * shares, axis=-1, keepdims=True)
    score_grad = (shares * (share_grad - centre)).astype(BF16)
    dq_ref[...] = (dot(score_grad, keys) * scale).astype(BF16)
    dk_ref[...] = (dot_rows(score_grad, queries) * scale).astype(BF16)
    dv_ref[...] = dot_rows(shares_low, upstream).astype(BF16)


def attend_backward(projected, pulled, mask, first_head):
    rows, wide = projected.shape
    head_dim = wide // 3 // HEADS
    count = pulled.shape[1] // head_dim
    block = (rows, head_dim)
    like = jax.ShapeDtypeStruct(pulled.shape, BF16)
    return pl.pallas_call(
        functools.partial(attend_backward_kernel, scale=head_dim**-0.5),
        grid_spec=pltpu.PrefetchScalarGridSpec(
            num_scalar_prefetch=1,
            grid=(count,),
            in_specs=[
                pl.BlockSpec(block, lambda h, f: (0, f[0] + h)),
                pl.BlockSpec(block, lambda h, f: (0, HEADS + f[0] + h)),
                pl.BlockSpec(block, lambda h, f: (0, 2 * HEADS + f[0] + h)),
                pl.BlockSpec(block, lambda h, f: (0, h)),
                pl.BlockSpec((rows, rows), lambda h, f: (0, 0)),
            ],
            out_specs=[pl.BlockSpec(block, lambda h, f: (0, h))] * 4,
        ),
        out_shape=[like] * 4,
        compiler_params=pltpu.CompilerParams(vmem_limit_bytes=48 * 2**20),
        name="attend_backward",
    )(first_head, projected, projected, projected, pulled, mask)


def column_kernel(
    cells_ref,
    upstream_ref,
    gain_ref,
    qkv_ref,
    qkv_t_ref,
    out_ref,
    out_t_ref,
    mix_gain_ref,
    up_ref,
    up_t_ref,
    down_ref,
    down_t_ref,
    result_ref,
    cells_grad_ref,
    gain_grad_ref,
    qkv_grad_ref,
    out_grad_ref,
    mix_gain_grad_ref,
    up_grad_ref,
    down_grad_ref,
    projected,
    normed_low,
    shares_kept,
    score_grads,
    mixed,
    mixed_grad,
    sum_grad,
    *,
    width,
    small,
):
    lanes = cells_ref.shape[1]
    heads = HEADS_ATTR
    scale = small**-0.5
    lane_blocks = lanes // 128
    gain = gain_ref[...]
    mix_gain = mix_gain_ref[...]

    for ref in (gain_grad_ref, qkv_grad_ref, out_grad_ref, mix_gain_grad_ref, up_grad_ref, down_grad_ref):
        ref[...] = jnp.zeros_like(ref)

    def at_rows(a):
        return pl.ds(pl.multiple_of(a * width, width), width)

    @pl.loop(0, ATTR)
    def _(a):
        normed, _ = normal_parts(cells_ref[at_rows(a), :].astype(F32), 0)
        low = (normed * gain).astype(BF16)
        normed_low[at_rows(a), :] = low
        projected[a] = dot(qkv_t_ref[...], low).astype(BF16).astype(F32).reshape(
            3, small, heads, lanes
        )

    for block in range(lane_blocks):
        here = slice(block * 128, block * 128 + 128)

        @pl.loop(0, ATTR)
        def _(a):
            query = projected[a, 0, :, :, here]
            scores = [
                jnp.sum(query * projected[b, 1, :, :, here], axis=0) * scale for b in range(ATTR)
            ]
            peak = functools.reduce(jnp.maximum, scores)
            lifted = [jnp.exp(score - peak) for score in scores]
            rate = 1.0 / functools.reduce(jnp.add, lifted)
            total = jnp.zeros((small, heads, 128), F32)
            for b in range(ATTR):
                share = lifted[b] * rate
                shares_kept[a, b, :, here] = share
                total += share.astype(BF16).astype(F32)[None] * projected[b, 2, :, :, here]
            mixed[at_rows(a), here] = total.reshape(width, 128).astype(BF16)

    @pl.loop(0, ATTR)
    def _(a):
        rows = at_rows(a)
        cells = cells_ref[rows, :].astype(F32)
        mixed_low = mixed[rows, :]
        third = (cells + dot(out_t_ref[...], mixed_low)).astype(BF16).astype(F32)
        normed, rate = normal_parts(third, 0)
        low = (normed * mix_gain).astype(BF16)
        hidden, slope = smooth_pair(dot(up_t_ref[...], low))
        hidden = hidden.astype(BF16)
        result_ref[rows, :] = (third + dot(down_t_ref[...], hidden)).astype(BF16)
        upstream = upstream_ref[rows, :]
        down_grad_ref[...] += dot_last(upstream, hidden)
        lifted_grad = (slope * dot(down_ref[...], upstream)).astype(BF16)
        up_grad_ref[...] += dot_last(low, lifted_grad)
        normed_grad = dot(up_ref[...], lifted_grad)
        mix_gain_grad_ref[...] += normed_grad * normed
        third_grad = (
            upstream.astype(F32) + normal_back(normed, rate, normed_grad * mix_gain, 0)
        ).astype(BF16)
        sum_grad[rows, :] = third_grad
        out_grad_ref[...] += dot_last(mixed_low, third_grad)
        mixed_grad[a] = dot(out_ref[...], third_grad).astype(BF16).astype(F32).reshape(
            small, heads, lanes
        )

    for block in range(lane_blocks):
        here = slice(block * 128, block * 128 + 128)

        @pl.loop(0, ATTR)
        def _(a):
            pulled = mixed_grad[a, :, :, here]
            share_grads = [
                jnp.sum(pulled * projected[b, 2, :, :, here], axis=0) for b in range(ATTR)
            ]
            shares = [shares_kept[a, b, :, here] for b in range(ATTR)]
            centre = functools.reduce(jnp.add, [s * g for s, g in zip(shares, share_grads)])
            total = jnp.zeros((small, heads, 128), F32)
            for b in range(ATTR):
                grad = (shares[b] * (share_grads[b] - centre)).astype(BF16).astype(F32)
                score_grads[a, b, :, here] = grad
                shares_kept[a, b, :, here] = shares[b].astype(BF16).astype(F32)
                total += grad[None] * projected[b, 1, :, :, here]
            mixed[at_rows(a), here] = (total * scale).reshape(width, 128).astype(BF16)

        @pl.loop(0, ATTR)
        def _(b):
            key_grad = jnp.zeros((small, heads, 128), F32)
            value_grad = jnp.zeros((small, heads, 128), F32)
            for a in range(ATTR):
                key_grad += score_grads[a, b, :, here][None] * projected[a, 0, :, :, here]
                value_grad += shares_kept[a, b, :, here][None] * mixed_grad[a, :, :, here]
            projected[b, 1, :, :, here] = key_grad * scale
            projected[b, 2, :, :, here] = value_grad

    @pl.loop(0, ATTR)
    def _(a):
        rows = at_rows(a)
        key_value = projected[a, 1:3].reshape(2 * width, lanes).astype(BF16)
        grads = jnp.concatenate([mixed[rows, :], key_value], axis=0)
        qkv_grad_ref[...] += dot_last(normed_low[rows, :], grads)
        normed_grad = dot(qkv_ref[...], grads)
        normed, rate = normal_parts(cells_ref[rows, :].astype(F32), 0)
        gain_grad_ref[...] += normed_grad * normed
        back = normal_back(normed, rate, normed_grad * gain, 0)
        cells_grad_ref[rows, :] = (sum_grad[rows, :].astype(F32) + back).astype(BF16)


def column_layers(cells, upstream, gain, qkv, out, mix_gain, up, down):
    depth, lanes = cells.shape
    width = depth // ATTR
    small = width // HEADS_ATTR
    hidden = up.shape[1]
    qkv_heads = qkv.reshape(width, 3, HEADS_ATTR, small).transpose(0, 1, 3, 2)
    qkv_heads = qkv_heads.reshape(width, 3 * width)
    out_heads = out.reshape(HEADS_ATTR, small, width).transpose(1, 0, 2).reshape(width, width)
    spread = functools.partial(jnp.broadcast_to, shape=(width, lanes))
    like = jax.ShapeDtypeStruct
    results = pl.pallas_call(
        functools.partial(column_kernel, width=width, small=small),
        out_shape=[
            like((depth, lanes), BF16),
            like((depth, lanes), BF16),
            like((width, lanes), F32),
            like((width, 3 * width), F32),
            like((width, width), F32),
            like((width, lanes), F32),
            like((width, hidden), F32),
            like((width, hidden), F32),
        ],
        scratch_shapes=[
            pltpu.VMEM((ATTR, 3, small, HEADS_ATTR, lanes), F32),
            pltpu.VMEM((depth, lanes), BF16),
            pltpu.VMEM((ATTR, ATTR, HEADS_ATTR, lanes), F32),
            pltpu.VMEM((ATTR, ATTR, HEADS_ATTR, lanes), F32),
            pltpu.VMEM((depth, lanes), BF16),
            pltpu.VMEM((ATTR, small, HEADS_ATTR, lanes), F32),
            pltpu.VMEM((depth, lanes), BF16),
        ],
        compiler_params=pltpu.CompilerParams(vmem_limit_bytes=48 * 2**20),
        name="column_layers",
    )(
        cells,
        upstream,
        spread(gain[:, None]),
        qkv_heads,
        qkv_heads.T,
        out_heads,
        out_heads.T,
        spread(mix_gain[:, None]),
        up,
        up.T,
        down,
        down.T,
    )
    result, cells_grad, gain_grad, qkv_grad, out_grad, mix_gain_grad, up_grad, down_grad = results
    qkv_grad = qkv_grad.reshape(width, 3, small, HEADS_ATTR).transpose(0, 1, 3, 2)
    out_grad = out_grad.reshape(small, HEADS_ATTR, width).transpose(1, 0, 2)
    return (
        result,
        cells_grad,
        jnp.sum(gain_grad, axis=1),
        qkv_grad.reshape(width, 3 * width),
        out_grad.reshape(width, width),
        jnp.sum(mix_gain_grad, axis=1),
        up_grad,
        down_grad.T,
    )


def one_bit(value, dim, bit):
    return lax.dynamic_index_in_dim(value, bit, dim, keepdims=False)


def halved(value, dim, own_bit, axis, mask):
    arrived = exchanged(one_bit(value, dim, 1 - own_bit).astype(BF16), axis, mask)
    return one_bit(value, dim, own_bit).astype(F32) + arrived.astype(F32)


def body(
    features,
    cotangent,
    row_counts,
    key_valid,
    attend_gain,
    attend_qkv,
    attend_out,
    mixer_gain,
    mixer_up,
    mixer_down,
    column_gain,
    column_qkv,
    column_out,
    column_mix_gain,
    column_up,
    column_down,
):
    dp_count = lax.axis_size("dp")
    section_count = lax.axis_size("section")
    dp_at, section_at = lax.axis_index("dp"), lax.axis_index("section")
    core, near, far = dp_at & 1, section_at & 1, section_at >> 1
    chip_bits = (dp_count // 2).bit_length() - 1
    group_rows, width = features.shape
    half_rows = group_rows // 2
    own = half_rows // 2
    head_dim = width // HEADS
    hidden = mixer_up.shape[1]

    counts = row_counts[0]
    bounds = jnp.cumsum(counts)
    largest = jnp.argmax(counts)
    start = bounds[largest] - counts[largest]
    half_start = start + half_rows * far
    own_start = half_start + own * near
    near_start = half_start + own * (1 - near)
    segment = jnp.sum(
        (lax.iota(jnp.int32, group_rows)[:, None] >= bounds[None, :]).astype(jnp.int32), axis=1
    )

    def turned(array):
        return jnp.concatenate([array, array[:half_rows]], axis=0)

    def cut(array, begin):
        return lax.dynamic_slice_in_dim(array, begin, own, 0)

    def both(array):
        longer = turned(array)
        return jnp.concatenate([cut(longer, own_start), cut(longer, near_start)], axis=0)

    half_x = both(features)
    half_segment, half_valid = both(segment), both(key_valid)
    upstream = cut(turned(cotangent), own_start)
    mask = (
        (half_segment[:, None] == half_segment[None, :])
        & ((half_valid == 1)[None, :] | jnp.eye(half_rows, dtype=bool))
    ).astype(F32)

    half_n, half_rate = normal_parts(half_x.astype(F32))
    half_normed = (half_n * attend_gain).astype(BF16)
    projected = dot(half_normed, attend_qkv).astype(BF16)
    attended = attend_forward(projected, mask, own)
    first = (half_x[:own].astype(F32) + dot(attended, attend_out)).astype(BF16)

    def across_cores(array):
        return jnp.concatenate([array, exchanged(array, "dp", 1)], axis=0)

    def across_near(array):
        return jnp.concatenate([array, exchanged(array, "section", 1)], axis=0)

    first_wide = first.astype(F32)
    second_n, second_rate = normal_parts(first_wide)
    second_normed = (second_n * mixer_gain).astype(BF16)
    hidden_own, slope_own = smooth_pair(dot(second_normed, mixer_up))
    second = (first_wide + dot(hidden_own.astype(BF16), mixer_down)).astype(BF16)

    part = hidden // (dp_count * section_count)

    def own_part(weight, dim):
        shape = weight.shape[:dim] + (dp_count // 2, 2, 2, 2, part) + weight.shape[dim + 1 :]
        taken = one_bit(one_bit(weight.reshape(shape), dim + 3, near), dim + 1, core)
        return taken.reshape(weight.shape[:dim] + (hidden // 4,) + weight.shape[dim + 1 :])

    up_part, down_part = own_part(mixer_up, 1), own_part(mixer_down, 0)
    pool_normed = across_cores(across_near(second_normed))
    pool_hidden, pool_slope = smooth_pair(dot(pool_normed, up_part))
    pool_hidden = pool_hidden.astype(BF16)

    columns = column_layers(
        second.T,
        upstream.T,
        column_gain,
        column_qkv,
        column_out,
        column_mix_gain,
        column_up,
        column_down,
    )
    result_own = columns[0].T
    second_grad = columns[1].T

    def to_columns(rows_own):
        quarter = width // section_count
        pieces = rows_own.reshape(own, section_count, quarter)
        kept = [one_bit(pieces, 1, section_at)]
        for mask_at in range(1, section_count):
            kept.append(exchanged(one_bit(pieces, 1, section_at ^ mask_at), "section", mask_at))
        stacked = jnp.stack(kept)
        ordered = jnp.take(stacked, jnp.arange(section_count) ^ section_at, axis=0)
        ordered = ordered.reshape(group_rows, quarter)
        doubled = jnp.concatenate([ordered, ordered], axis=0)
        return lax.dynamic_slice_in_dim(doubled, group_rows - start, group_rows, 0)

    result = to_columns(result_own)

    def summed(flat):
        for mask_at in [1 << bit for bit in range(chip_bits + 1)]:
            flat = flat + exchanged(flat, "dp", mask_at)
        for mask_at in (1, 2):
            flat = flat + exchanged(flat, "section", mask_at)
        return flat

    small_grads = columns[2:]
    small_sum = summed(jnp.concatenate([grad.reshape(-1) for grad in small_grads]))

    lifted_grad = (slope_own * dot_last(second_grad, mixer_down)).astype(BF16)
    second_normed_grad = dot_last(lifted_grad, mixer_up)
    mixer_gain_grad = jnp.sum(second_normed_grad * second_n, axis=0)
    back = normal_back(second_n, second_rate, second_normed_grad * mixer_gain)
    first_grad = (second_grad.astype(F32) + back).astype(BF16)

    pool_grad = across_cores(across_near(second_grad))
    down_grad = dot_rows(pool_hidden, pool_grad)
    pool_lifted = (pool_slope * dot_last(pool_grad, down_part)).astype(BF16)
    up_grad = dot_rows(pool_normed, pool_lifted)

    def scattered(grad):
        bits = (2,) * (chip_bits + 1)
        rest, columns_all = grad.shape[0] >> (chip_bits + 1), grad.shape[1]
        shaped = grad.reshape(bits + (rest, columns_all))
        done = []
        for piece, order in (
            (shaped[..., : columns_all // 2], range(chip_bits)),
            (shaped[..., columns_all // 2 :], range(chip_bits - 1, -1, -1)),
        ):
            left = list(range(chip_bits))
            for bit in order:
                dim = left.index(chip_bits - 1 - bit)
                left.pop(dim)
                piece = halved(piece, dim, (dp_at >> (bit + 1)) & 1, "dp", 2 << bit)
            done.append(halved(piece, 0, far, "section", 2))
        return jnp.concatenate(done, axis=-1)

    def quad_columns(block):
        low = block.astype(BF16).reshape((2, 2) + block.shape[1:])
        rows_near = one_bit(low, 1, near)
        other = exchanged(one_bit(low, 1, 1 - near), "section", 1)
        pair = jnp.where(near == 0, jnp.stack([rows_near, other]), jnp.stack([other, rows_near]))
        rows_core = one_bit(pair, 1, core)
        other = exchanged(one_bit(pair, 1, 1 - core), "dp", 1)
        quad = jnp.where(core == 0, jnp.stack([rows_core, other]), jnp.stack([other, rows_core]))
        return quad.transpose(2, 0, 1, 3).astype(F32)

    mixer_down_grad = scattered(down_grad)

    def rows_first(grad):
        rows, cols = grad.shape
        rest = rows // (dp_count * section_count)
        shaped = grad.reshape(dp_count // 2, 2, 2, 2, rest, cols).transpose(0, 2, 1, 3, 4, 5)
        return shaped.reshape(rows, cols), rest

    ordered, rest = rows_first(up_grad)
    up_block = quad_columns(scattered(ordered).reshape(4, rest, hidden // 4))
    mixer_up_grad = (
        up_block.reshape(rest, 2, 2, dp_count // 2, 2, part)
        .transpose(0, 3, 1, 4, 2, 5)
        .reshape(rest, hidden)
    )

    own_heads = HEADS // 2
    own_width = own_heads * head_dim
    first_head = (near * own_heads).astype(jnp.int32)
    half_grad = across_near(first_grad)
    own_out = lax.dynamic_slice_in_dim(attend_out, near * own_width, own_width, 0)
    half_pulled = dot_last(half_grad, own_out).astype(BF16)
    half_mixed, dq, dk, dv = attend_backward(projected, half_pulled, mask, first_head[None])
    half_dqkv = jnp.stack([dq, dk, dv], axis=1)
    own_qkv = lax.dynamic_slice_in_dim(
        attend_qkv.reshape(width, 3, width), near * own_width, own_width, 2
    )
    qkv_in_grad = dot_last(
        half_dqkv.reshape(half_rows, 3 * own_width), own_qkv.reshape(width, 3 * own_width)
    )
    arrived = exchanged(qkv_in_grad[own:].astype(BF16), "section", 1)
    normed_grad = qkv_in_grad[:own] + arrived.astype(F32)
    own_n, own_rate = half_n[:own], half_rate[:own]
    attend_gain_grad = jnp.sum(normed_grad * own_n, axis=0)
    back = normal_back(own_n, own_rate, normed_grad * attend_gain)
    input_own = (first_grad.astype(F32) + back).astype(BF16)
    input_grad = to_columns(input_own).astype(F32)

    def core_heads(array):
        shaped = array.reshape(array.shape[:-1] + (2, own_width // 2))
        dim = shaped.ndim - 2
        arrived = exchanged(one_bit(shaped, dim, 1 - core), "dp", 1)
        return jnp.concatenate([one_bit(shaped, dim, core), arrived], axis=0)

    pool_dqkv = core_heads(half_dqkv).reshape(group_rows, 3 * own_width // 2)
    pool_first = across_cores(half_normed)
    qkv_grad = dot_rows(pool_first, pool_dqkv)
    ordered, rest = rows_first(qkv_grad)
    qkv_block = quad_columns(scattered(ordered).reshape(4, rest, 3 * own_width // 2))
    attend_qkv_grad = (
        qkv_block.reshape(rest, 2, 2, 3, own_width // 2)
        .transpose(0, 3, 2, 1, 4)
        .reshape(rest, 3 * width)
    )

    pool_mixed = core_heads(half_mixed)
    pool_first_grad = across_cores(half_grad)
    out_grad = dot_rows(pool_mixed, pool_first_grad)
    out_block = scattered(out_grad)
    moves = []
    blocks = dp_count * section_count
    per_quad = blocks // 4
    for dp_from in range(dp_count):
        for section_from in range(section_count):
            place = (dp_from >> 1) * 2 + (section_from >> 1)
            holds = ((section_from & 1) * 2 + (dp_from & 1)) * per_quad + place
            moves.append((dp_from * section_count + section_from, holds))
    attend_out_grad = lax.ppermute(out_block.astype(BF16), ("dp", "section"), moves).astype(F32)

    gains = summed(jnp.stack([attend_gain_grad, mixer_gain_grad]))
    share = width // (dp_count * section_count)
    gains = lax.dynamic_slice_in_dim(gains, (dp_at * section_count + section_at) * share, share, 1)

    small_out, at = [], 0
    for grad in small_grads:
        small_out.append(small_sum[at : at + grad.size].reshape(grad.shape))
        at += grad.size
    return (
        result,
        input_grad,
        gains[0],
        attend_qkv_grad,
        attend_out_grad,
        gains[1],
        mixer_up_grad,
        mixer_down_grad,
        *small_out,
    )


def solution(mesh):
    split = P(("dp", "section"))
    return jax.shard_map(
        body,
        mesh=mesh,
        in_specs=(P("dp", None), P("dp", None), P("dp", None), P("dp")) + (P(),) * 12,
        out_specs=(P("dp", "section"),) * 2 + (split,) * 6 + (P(),) * 6,
        check_vma=False,
    )
```

time: 3650 us -> 416 us (0.11)
  waiting for transfers between devices: 2060 us -> 77.9 us
  starting transfers between devices: 1050 us -> 63.7 us
  loops' own time: 169 us -> 0 us
  local copies, waits for them, and re-layouts: 210 us -> 94.1 us
  Pallas kernels: 0 us -> 45.3 us
    reduce_scatter x4 -> x0, waiting for transfers between devices: 1040 us -> none  [the longest x1 366 us: body(): lax.psum_scatter(gradients[4], ('dp', 'section'), scatter_dimension=0, ti...]
    ppermute x14 -> x55, starting transfers between devices: 1050 us -> 63.7 us  [the longest x54 63 us: exchanged(): return lax.ppermute(value, axis, [(at, at ^ mask) for at in range(count)])]
    ppermute x14 -> x55, waiting for transfers between devices: 485 us -> 77.9 us  [the longest x54 77.9 us: exchanged(): return lax.ppermute(value, axis, [(at, at ^ mask) for at in range(count)])]
    psum x2 -> x0, waiting for transfers between devices: 283 us -> none  [the longest x1 156 us: broadcast(): return lax.psum(kept, axis)]
    unnamed x8 -> x0, waiting for transfers between devices: 254 us -> none
    another operation x21 -> x0, loops' own time: 169 us -> none  [the longest x4 117 us: backward_run(): return lax.switch(section_at, backward_branches, *operands)]
    pallas_call x0 -> x3, Pallas kernels: none -> 45.3 us  [the longest x1 31.4 us: column_layers(): pl.pallas_call(functools.partial(column_kernel, width=width, small=small)...]
  transfers between devices with their start and end apart: 21 -> 55, of which waited for: 21 -> 20; matrix products, arithmetic and copies ran while one was open for 2% -> 35% of each run, Pallas kernels for 0% -> 2%
where the time goes in v1:
time: 416 us; the launch traced here: 410 us
  local copies, waits for them, and re-layouts  94.1 us (23%)
  waiting for transfers between devices  77.9 us (19%)
  matrix products  69.8 us (17%)
  starting transfers between devices  63.7 us (15%)
  other arithmetic  52.5 us (13%)
  Pallas kernels  45.3 us (11%)
  between operations  6.49 us (2%)
    ppermute x54, waiting for transfers between devices, exchanged(): return lax.ppermute(value, axis, [(at, at ^ mask) for at in range(count)])  77.9 us
    ppermute x54, starting transfers between devices, exchanged(): return lax.ppermute(value, axis, [(at, at ^ mask) for at in range(count)])  63 us
    unnamed x127, local copies, waits for them, and re-layouts  37.9 us
    pallas_call x1, Pallas kernels, column_layers(): pl.pallas_call(functools.partial(column_kernel, width=width, small=small)...  31.4 us
    dot_general x5, matrix products, dot(): return jnp.dot(left, right, preferred_element_type=F32)  28.2 us
    dot_general x4, matrix products, dot_rows(): lax.dot_general(left, right, (((0,), (0,)), ((), ())), preferred_element_...  21.3 us
    dot_general x3, matrix products, dot_last(): lax.dot_general(left, right, (((1,), (1,)), ((), ())), preferred_element_...  20.3 us
    dynamic_slice x15, local copies, waits for them, and re-layouts, one_bit(): return lax.dynamic_index_in_dim(value, bit, dim, keepdims=False)  18.5 us
  transfers between devices with their start and end apart: 55, of which 20 were waited for; matrix products, arithmetic and copies ran while one was open for 35% of the time, Pallas kernels for 2%

profile of v1, /device:TPU:0, one launch (start us, length us, event | category | flops | bytes accessed | tf_op | source)
XLA Modules:
  0.0 409.7 jit_solution(2224859085411690231)
XLA Ops:
  8.0 3.9 copy.145
  12.0 4.0 copy.150
  16.0 2.3 slice.125
  18.3 3.9 fusion.66
  24.5 6.9 %convolution_convert_fusion.q_ref.k_ref.v_ref = bf16[512,3072]{1,0:T(8,128)(2,1)S(1)} fusion(bf16[512,1024]{0,1:T(8,128)(2,1)S(1)} %get-tuple-element.100, bf16[1024,3072]{1,0:T(8,128)(2,1)} %param.23), kind=kOutput, calls=%fused_computation.4 | convolution fusion | flops 3222798336 | bytes 10485760 | tf_op jit(solution)/shard_map/dot_general | solution.py:55
  31.8 5.7 %attend_forward.1 = bf16[256,1024]{1,0:T(8,128)(2,1)S(1)} custom-call(bf16[512,3072]{1,0:T(8,128)(2,1)S(1)} %convolution_convert_fusion.q_ref.k_ref.v_ref, bf16[512,3072]{1,0:T(8,128)(2,1)S(1)} %convolution_convert_fusion.q_ref.k_ref.v_ref, bf16[512,3072]{1,0:T(8,128)(2,1)S(1)} %convolution_convert_fusion.q_ref.k_ref.v_ref, f32[512,512]{1,0:T(8,128)S(1)} %fusion.52.mask_ref), custom_call_target="tpu_custom_call" | custom-call | tf_op jit(solution)/shard_map/attend_forward/pallas_call | solution.py:77
  42.2 5.8 %fusion.138 = f32[256,4096]{1,0:T(8,128)S(1)} fusion(bf16[256,1024]{0,1:T(8,128)(2,1)S(1)} %fusion.41, bf16[1024,4096]{1,0:T(8,128)(2,1)} %param.26), kind=kOutput, calls=%fused_computation.301 | convolution fusion | flops 2147483648 | bytes 13107200 | tf_op jit(solution)/shard_map/dot_general | solution.py:55
  48.1 8.8 %fusion.40.cells_ref = bf16[1024,256]{1,0:T(8,128)(2,1)S(1)} fusion(bf16[4096,1024]{1,0:T(8,128)(2,1)} %param.27, f32[256,4096]{1,0:T(8,128)S(1)} %fusion.138, bf16[256,1024]{0,1:T(8,128)(2,1)S(1)} %copy-done.24), kind=kOutput, calls=%fused_computation.69 | convolution fusion | flops 2157707264 | bytes 13631488 | tf_op jit(solution)/shard_map/dot_general | solution.py:55
  57.1 31.4 %column_layers.1 = (bf16[1024,256]{1,0:T(8,128)(2,1)S(1)}, bf16[1024,256]{1,0:T(8,128)(2,1)S(1)}, f32[64,256]{1,0:T(8,128)S(1)}, f32[64,192]{1,0:T(8,128)S(1)}, ...) custom-call(bf16[1024,256]{1,0:T(8,128)(2,1)S(1)} %fusion.40.cells_ref, ...), custom_call_target="tpu_custom_call" | custom-call | tf_op jit(solution)/shard_map/column_layers/pallas_call | solution.py:287
  92.6 14.5 %fusion.47 = (f32[1024]{0:T(1024)S(1)}, f32[256]{0:T(256)S(1)}, f32[256]{0:T(256)S(1)}, f32[256,1024]{0,1:T(8,128)}) fusion(bf16[256,1024]{0,1:T(8,128)(2,1)} %copy-done.23, f32[256]{0:T(256)} %copy-done.52, f32[256]{0:T(256)} %copy-done.46, f32[1024]{0:T(1024)} %param.25, bf16[1024,4096]{1,0:T(8,128)(2,1)} %param.26, bf16[1024,256]{1,0:T(8,128)(2,1)} %copy-done.4, ...), kind=kOutput, calls=%fused_computation.76 | convolution fusion | flops 4315151360 | bytes 23080960 | tf_op jit(solution)/shard_map/dot_general | solution.py:63
  107.2 2.7 fusion.46
  110.0 3.0 collective-permute-start.3
  116.5 2.1 collective-permute-start.2
  122.0 2.2 collective-permute-start
  125.0 2.1 copy.189
  129.2 12.0 %copy.184 = bf16[1024,4096]{0,1:T(8,128)(2,1)} copy(bf16[1024,4096]{1,0:T(8,128)(2,1)} %param.26) | data formatting | bytes 16777216 | tf_op args[8]
  141.2 3.1 constant_dynamic-slice_fusion.1
  144.2 3.1 constant_dynamic-slice_fusion
  147.3 8.6 %copy.163 = bf16[1024,3072]{0,1:T(8,128)(2,1)} copy(bf16[1024,3072]{1,0:T(8,128)(2,1)} %param.23) | data formatting | bytes 12582912 | tf_op args[5]
  161.3 2.0 collective-permute-start.34
  163.4 2.0 pad_maximum_fusion.13
  165.3 2.4 gather_fusion
  169.9 1.9 convolution_convert_fusion.1.up_ref
  171.9 8.2 %attend_backward.1 = (bf16[512,512]{1,0:T(8,128)(2,1)S(1)}, bf16[512,512]{1,0:T(8,128)(2,1)S(1)}, bf16[512,512]{1,0:T(8,128)(2,1)S(1)}, bf16[512,512]{1,0:T(8,128)(2,1)S(1)}) custom-call(s32[1]{0:T(128)} %bitcast.28.first_ref, bf16[512,3072]{1,0:T(8,128)(2,1)} %copy-done.2, bf16[512,3072]{1,0:T(8,128)(2,1)} %copy-done.2, bf16[512,3072]{1,0:T(8,128)(2,1)} %copy-done.2, ...), custom_call_target="tpu_custom_call" | custom-call | tf_op jit(solution)/shard_map/attend_backward/pallas_call | solution.py:116
  181.5 3.8 fusion.22
  190.9 2.1 constant_dynamic-slice_fusion.3
  194.1 2.3 pad_maximum_fusion.5
  196.4 7.7 %collective-permute-done.53 = f32[49280]{0:T(1024)} collective-permute-done((f32[49280]{0:T(1024)S(1)}, f32[49280]{0:T(1024)}, u32[]{:S(2)}, u32[]{:S(2)}) %collective-permute-start.53) | collective-permute-done | bytes 197152 | tf_op jit(solution)/shard_map/ppermute | solution.py:24
  206.8 2.2 pad_maximum_fusion.6
  211.2 2.1 pad_maximum_fusion.7
  213.3 4.4 %collective-permute-done.54 = f32[49280]{0:T(1024)} collective-permute-done((f32[49280]{0:T(1024)S(1)}, f32[49280]{0:T(1024)}, u32[]{:S(2)}, u32[]{:S(2)}) %collective-permute-start.54) | collective-permute-done | bytes 197152 | tf_op jit(solution)/shard_map/ppermute | solution.py:24
  222.2 2.2 multiply_reduce_fusion
  226.3 3.1 collective-permute-done.9
  230.0 2.2 add_convert_fusion
  233.3 2.7 collective-permute-start.7
  238.0 2.3 collective-permute-start.12
  240.3 2.8 pad_maximum_fusion
  243.3 3.4 collective-permute-done.12
  248.5 3.2 collective-permute-done.5
  254.0 2.2 fusion.61
  256.3 2.3 fusion.62
  261.1 3.8 convolution_bitcast_fusion
  269.3 2.5 fusion.8
  275.3 5.8 %fusion.55 = f32[1024,1024]{1,0:T(8,128)} fusion(bf16[1024,1024]{0,1:T(8,128)(2,1)S(1)} %bitcast.303, bf16[512,1024]{0,1:T(8,128)(2,1)} %collective-permute-done.33, bf16[256,1024]{0,1:T(8,128)(2,1)} %collective-permute-done.32, bf16[256,1024]{0,1:T(8,128)(2,1)S(1)} %copy-done.18), kind=kOutput, calls=%fused_computation.108 | convolution fusion | flops 2153775104 | bytes 8388608 | tf_op jit(solution)/shard_map/dot_general | solution.py:55
  281.1 10.6 %fusion.53 = f32[1024,1024]{1,0:T(8,128)} fusion(f32[1024,1024]{1,0:T(8,128)} %fusion.55, bf16[1024,1024]{1,0:T(8,128)(2,1)} %bitcast.302, bf16[512,1024]{0,1:T(8,128)(2,1)} %collective-permute-done.35, bf16[256,1024]{0,1:T(8,128)(2,1)} %collective-permute-done.34, bf16[256,1024]{0,1:T(8,128)(2,1)S(1)} %bitcast.278, ...), kind=kOutput, calls=%fused_computation.106 | convolution fusion | flops 4325376000 | bytes 14680064 | tf_op jit(solution)/shard_map/dot_general | solution.py:59
  291.7 2.5 copy.185
  296.5 4.4 %fusion.7 = f32[1024,1024]{1,0:T(8,128)S(1)} fusion(f32[1024,1024]{1,0:T(8,128)S(1)} %copy-done.57, bf16[512,1024]{0,1:T(8,128)(2,1)} %collective-permute-done.35, bf16[256,1024]{0,1:T(8,128)(2,1)} %collective-permute-done.34, bf16[256,1024]{0,1:T(8,128)(2,1)S(1)} %bitcast.279), kind=kOutput, calls=%fused_computation.26 | convolution fusion | flops 2163212288 | bytes 10485760 | tf_op jit(solution)/shard_map/dot_general | solution.py:59
  309.6 10.9 %collective-permute-done.29 = bf16[2,32,512]{2,1,0:T(8,128)(2,1)S(1)} collective-permute-done((bf16[2,32,512]{2,1,0:T(8,128)(2,1)S(1)}, bf16[2,32,512]{2,1,0:T(8,128)(2,1)S(1)}, u32[]{:S(2)}, u32[]{:S(2)}) %collective-permute-start.29) | collective-permute-done | bytes 65568 | tf_op jit(solution)/shard_map/ppermute | solution.py:24
  322.1 2.7 collective-permute-done.26
  326.0 4.3 %collective-permute-done.30 = bf16[32,512]{1,0:T(8,128)(2,1)S(1)} collective-permute-done((bf16[32,512]{1,0:T(8,128)(2,1)S(1)}, bf16[32,512]{1,0:T(8,128)(2,1)S(1)}, u32[]{:S(2)}, u32[]{:S(2)}) %collective-permute-start.30) | collective-permute-done | bytes 32800 | tf_op jit(solution)/shard_map/ppermute | solution.py:24
  331.0 4.1 %collective-permute-done.27 = bf16[32,512]{1,0:T(8,128)(2,1)S(1)} collective-permute-done((bf16[32,512]{1,0:T(8,128)(2,1)S(1)}, bf16[32,512]{1,0:T(8,128)(2,1)S(1)}, u32[]{:S(2)}, u32[]{:S(2)}) %collective-permute-start.27) | collective-permute-done | bytes 32800 | tf_op jit(solution)/shard_map/ppermute | solution.py:24
  335.9 5.4 %collective-permute-start.44 = (bf16[2,2,128,512]{3,2,1,0:T(8,128)(2,1)S(1)}, bf16[2,2,128,512]{3,2,1,0:T(8,128)(2,1)S(1)}, u32[]{:S(2)}, u32[]{:S(2)}) collective-permute-start(bf16[2,2,128,512]{3,2,1,0:T(8,128)(2,1)S(1)} %fusion.57), channel_id=1, source_target_pairs={{0,8},{4,12},{8,0},{12,4},{16,24},{20,28},{24,16},{28,20},{1,9},{5... | collective-permute-start | bytes 1572872 | tf_op jit(solution)/shard_map/ppermute | solution.py:24
  342.0 3.3 collective-permute-start.16
  345.3 3.6 collective-permute-done.16
  350.5 3.9 collective-permute-done.20
  356.1 3.8 collective-permute-done.17
  360.0 3.5 collective-permute-start.21
  367.4 2.1 collective-permute-start.37
  377.0 2.3 collective-permute-start.41
  382.4 2.3 collective-permute-start.49
  386.5 9.1 %collective-permute-done.41 = bf16[128,512]{1,0:T(8,128)(2,1)S(1)} collective-permute-done((bf16[128,512]{1,0:T(8,128)(2,1)S(1)}, bf16[128,512]{1,0:T(8,128)(2,1)S(1)}, u32[]{:S(2)}, u32[]{:S(2)}) %collective-permute-start.41) | collective-permute-done | bytes 131104 | tf_op jit(solution)/shard_map/ppermute | solution.py:24
  395.6 2.8 collective-permute-done.38
  398.6 2.7 collective-permute-done.49
  401.4 4.3 %collective-permute-done.42 = bf16[2,32,1024]{2,1,0:T(8,128)(2,1)S(1)} collective-permute-done((bf16[2,32,1024]{2,1,0:T(8,128)(2,1)S(1)}, bf16[2,32,1024]{2,1,0:T(8,128)(2,1)S(1)}, u32[]{:S(2)}, u32[]{:S(2)}) %collective-permute-start.42) | collective-permute-done | bytes 131104 | tf_op jit(solution)/shard_map/ppermute | solution.py:24
  (369 shorter events, 109.1 us)
Async XLA Ops:
  0.6 36.9 %copy-start = (bf16[1024,1024]{1,0:T(8,128)(2,1)S(1)}, bf16[1024,1024]{1,0:T(8,128)(2,1)}, u32[]{:S(2)}) copy-start(bf16[1024,1024]{1,0:T(8,128)(2,1)} %param.24) | copy-start | bytes 6291460
  107.1 17.1 %copy-start.16 = (f32[64,192]{1,0:T(8,128)S(1)}, f32[64,192]{1,0:T(8,128)}, u32[]{:S(2)}) copy-start(f32[64,192]{1,0:T(8,128)} %copy-done.15) | copy-start | bytes 147460
  107.2 21.4 %copy-start.14 = (f32[64,256]{1,0:T(8,128)S(1)}, f32[64,256]{1,0:T(8,128)}, u32[]{:S(2)}) copy-start(f32[64,256]{1,0:T(8,128)} %copy-done.13) | copy-start | bytes 196612
  107.2 21.5 %copy-start.12 = (f32[64,256]{1,0:T(8,128)S(1)}, f32[64,256]{1,0:T(8,128)}, u32[]{:S(2)}) copy-start(f32[64,256]{1,0:T(8,128)} %copy-done.11) | copy-start | bytes 196612
  107.2 21.6 %copy-start.10 = (f32[64,256]{1,0:T(8,128)S(1)}, f32[64,256]{1,0:T(8,128)}, u32[]{:S(2)}) copy-start(f32[64,256]{1,0:T(8,128)} %copy-done.9) | copy-start | bytes 196612
  110.0 60.0 %collective-permute-start.3 = (bf16[256,1024]{0,1:T(8,128)(2,1)}, bf16[256,1024]{0,1:T(8,128)(2,1)}, u32[]{:S(2)}, u32[]{:S(2)}) collective-permute-start(bf16[256,1024]{0,1:T(8,128)(2,1)} %fusion.46), channel_id=1, source_target_pairs={{0,1},{1,0},{2,3},{3,2},{4,5},{5,4},{6,7},{7,6},{8,9},{9,8},{10,11... | collective-permute-start | bytes 1572872 | tf_op jit(solution)/shard_map/ppermute | solution.py:24
  116.5 44.6 %collective-permute-start.2 = (bf16[256,256]{1,0:T(8,128)(2,1)}, bf16[256,256]{1,0:T(8,128)(2,1)}, u32[]{:S(2)}, u32[]{:S(2)}) collective-permute-start(bf16[256,256]{1,0:T(8,128)(2,1)} %bitcast.328), channel_id=1, source_target_pairs={{0,3},{1,2},{2,1},{3,0},{4,7},{5,6},{6,5},{7,4},{8,11},{9,10},{10,... | collective-permute-start | bytes 393224 | tf_op jit(solution)/shard_map/ppermute | solution.py:24
  120.3 41.0 %collective-permute-start.1 = (bf16[256,256]{1,0:T(8,128)(2,1)}, bf16[256,256]{1,0:T(8,128)(2,1)}, u32[]{:S(2)}, u32[]{:S(2)}) collective-permute-start(bf16[256,256]{1,0:T(8,128)(2,1)} %bitcast.327), channel_id=1, source_target_pairs={{0,2},{1,3},{2,0},{3,1},{4,6},{5,7},{6,4},{7,5},{8,10},{9,11},{10,... | collective-permute-start | bytes 393224 | tf_op jit(solution)/shard_map/ppermute | solution.py:24
  122.0 39.3 %collective-permute-start = (bf16[256,256]{1,0:T(8,128)(2,1)}, bf16[256,256]{1,0:T(8,128)(2,1)}, u32[]{:S(2)}, u32[]{:S(2)}) collective-permute-start(bf16[256,256]{1,0:T(8,128)(2,1)} %bitcast.326), channel_id=1, source_target_pairs={{0,1},{1,0},{2,3},{3,2},{4,5},{5,4},{6,7},{7,6},{8,9},{9,8},{10,11... | collective-permute-start | bytes 393224 | tf_op jit(solution)/shard_map/ppermute | solution.py:24
  129.1 29.0 %collective-permute-start.50 = (f32[49280]{0:T(1024)S(1)}, f32[49280]{0:T(1024)}, u32[]{:S(2)}, u32[]{:S(2)}) collective-permute-start(f32[49280]{0:T(1024)S(1)} %concatenate.109), channel_id=1, source_target_pairs={{0,4},{4,0},{8,12},{12,8},{16,20},{20,16},{24,28},{28,24},{1,5},{5... | collective-permute-start | bytes 591368 | tf_op jit(solution)/shard_map/ppermute | solution.py:24
  159.0 8.7 %collective-permute-start.51 = (f32[49280]{0:T(1024)S(1)}, f32[49280]{0:T(1024)S(1)}, u32[]{:S(2)}, u32[]{:S(2)}) collective-permute-start(f32[49280]{0:T(1024)S(1)} %add.418), channel_id=1, source_target_pairs={{0,8},{4,12},{8,0},{12,4},{16,24},{20,28},{24,16},{28,20},{1,9},{5... | collective-permute-start | bytes 591368 | tf_op jit(solution)/shard_map/ppermute | solution.py:24
  161.1 76.9 %collective-permute-start.13 = (bf16[512,1024]{0,1:T(8,128)(2,1)}, bf16[512,1024]{0,1:T(8,128)(2,1)}, u32[]{:S(2)}, u32[]{:S(2)}) collective-permute-start(bf16[512,1024]{0,1:T(8,128)(2,1)} %copy-done.26), channel_id=1, source_target_pairs={{0,4},{4,0},{8,12},{12,8},{16,20},{20,16},{24,28},{28,24},{1,5},{5... | collective-permute-start | bytes 3145736 | tf_op jit(solution)/shard_map/ppermute | solution.py:24
  161.3 43.8 %collective-permute-start.32 = (bf16[256,1024]{0,1:T(8,128)(2,1)}, bf16[256,1024]{0,1:T(8,128)(2,1)}, u32[]{:S(2)}, u32[]{:S(2)}) collective-permute-start(bf16[256,1024]{0,1:T(8,128)(2,1)} %copy-done.17), channel_id=1, source_target_pairs={{0,1},{1,0},{2,3},{3,2},{4,5},{5,4},{6,7},{7,6},{8,9},{9,8},{10,11... | collective-permute-start | bytes 1572872 | tf_op jit(solution)/shard_map/ppermute | solution.py:24
  161.3 49.7 %collective-permute-start.34 = (bf16[256,1024]{0,1:T(8,128)(2,1)}, bf16[256,1024]{0,1:T(8,128)(2,1)}, u32[]{:S(2)}, u32[]{:S(2)}) collective-permute-start(bf16[256,1024]{0,1:T(8,128)(2,1)} %bitcast.276), channel_id=1, source_target_pairs={{0,1},{1,0},{2,3},{3,2},{4,5},{5,4},{6,7},{7,6},{8,9},{9,8},{10,11... | collective-permute-start | bytes 1572872 | tf_op jit(solution)/shard_map/ppermute | solution.py:24
  168.4 19.6 %collective-permute-start.52 = (f32[49280]{0:T(1024)}, f32[49280]{0:T(1024)}, u32[]{:S(2)}, u32[]{:S(2)}) collective-permute-start(f32[49280]{0:T(1024)} %add.419), channel_id=1, source_target_pairs={{0,16},{4,20},{8,24},{12,28},{16,0},{20,4},{24,8},{28,12},{1,17},{... | collective-permute-start | bytes 591368 | tf_op jit(solution)/shard_map/ppermute | solution.py:24
  186.3 36.0 %collective-permute-start.4 = (bf16[256,1024]{0,1:T(8,128)(2,1)}, bf16[256,1024]{0,1:T(8,128)(2,1)}, u32[]{:S(2)}, u32[]{:S(2)}) collective-permute-start(bf16[256,1024]{0,1:T(8,128)(2,1)} %slice.158), channel_id=1, source_target_pairs={{0,1},{1,0},{2,3},{3,2},{4,5},{5,4},{6,7},{7,6},{8,9},{9,8},{10,11... | collective-permute-start | bytes 1572872 | tf_op jit(solution)/shard_map/ppermute | solution.py:24
  189.1 17.7 %copy-start.18 = (bf16[256,1024]{0,1:T(8,128)(2,1)S(1)}, bf16[256,1024]{0,1:T(8,128)(2,1)}, u32[]{:S(2)}) copy-start(bf16[256,1024]{0,1:T(8,128)(2,1)} %copy-done.17) | copy-start | bytes 1572868
  189.2 15.0 %collective-permute-start.53 = (f32[49280]{0:T(1024)S(1)}, f32[49280]{0:T(1024)}, u32[]{:S(2)}, u32[]{:S(2)}) collective-permute-start(f32[49280]{0:T(1024)S(1)} %add.420), channel_id=1, source_target_pairs={{0,1},{1,0},{2,3},{3,2},{4,5},{5,4},{6,7},{7,6},{8,9},{9,8},{10,11... | collective-permute-start | bytes 591368 | tf_op jit(solution)/shard_map/ppermute | solution.py:24
  194.1 16.1 %copy-start.38 = (bf16[512,1,256]{2,1,0:T(2,128)(2,1)S(1)}, bf16[512,1,256]{2,1,0:T(2,128)(2,1)}, u32[]{:S(2)}) copy-start(bf16[512,1,256]{2,1,0:T(2,128)(2,1)} %get-tuple-element.104) | copy-start | bytes 786436
  194.1 16.1 %copy-start.37 = (bf16[512,1,256]{2,1,0:T(2,128)(2,1)S(1)}, bf16[512,1,256]{2,1,0:T(2,128)(2,1)}, u32[]{:S(2)}) copy-start(bf16[512,1,256]{2,1,0:T(2,128)(2,1)} %get-tuple-element.103) | copy-start | bytes 786436
  204.2 54.4 %collective-permute-start.14 = (bf16[512,3,256]{2,0,1:T(8,128)(2,1)}, bf16[512,3,256]{2,0,1:T(8,128)(2,1)}, u32[]{:S(2)}, u32[]{:S(2)}) collective-permute-start(bf16[512,3,256]{2,0,1:T(8,128)(2,1)} %bitcast.315), channel_id=1, source_target_pairs={{0,4},{4,0},{8,12},{12,8},{16,20},{20,16},{24,28},{28,24},{1,5},{5... | collective-permute-start | bytes 2359304 | tf_op jit(solution)/shard_map/ppermute | solution.py:24
  205.1 12.6 %collective-permute-start.54 = (f32[49280]{0:T(1024)S(1)}, f32[49280]{0:T(1024)}, u32[]{:S(2)}, u32[]{:S(2)}) collective-permute-start(f32[49280]{0:T(1024)S(1)} %add.421), channel_id=1, source_target_pairs={{0,2},{1,3},{2,0},{3,1},{4,6},{5,7},{6,4},{7,5},{8,10},{9,11},{10,... | collective-permute-start | bytes 591368 | tf_op jit(solution)/shard_map/ppermute | solution.py:24
  211.0 19.0 %slice-start.1 = ((f32[512]{0:T(512)}), f32[256]{0:T(256)S(1)}, s32[]{:S(2)}) async-start(f32[512]{0:T(512)} %copy-done.51), calls=%async_computation.1 | async-start | bytes 2048 | tf_op jit(solution)/shard_map/slice | solution.py:543
  211.0 58.3 %collective-permute-start.24 = (bf16[512,1024]{0,1:T(8,128)(2,1)}, bf16[512,1024]{0,1:T(8,128)(2,1)}, u32[]{:S(2)}, u32[]{:S(2)}) collective-permute-start(bf16[512,1024]{0,1:T(8,128)(2,1)} %pad_maximum_fusion.5), channel_id=1, source_target_pairs={{0,4},{4,0},{8,12},{12,8},{16,20},{20,16},{24,28},{28,24},{1,5},{5... | collective-permute-start | bytes 3145736 | tf_op jit(solution)/shard_map/ppermute | solution.py:24
  224.4 1.2 collective-permute-start.8
  225.7 3.7 collective-permute-start.9
  229.4 3.7 collective-permute-start.10
  233.1 4.1 %collective-permute-start.11 = (f32[2,1024]{1,0:T(2,128)S(1)}, f32[2,1024]{1,0:T(2,128)S(1)}, u32[]{:S(2)}, u32[]{:S(2)}) collective-permute-start(f32[2,1024]{1,0:T(2,128)S(1)} %add.375), channel_id=1, source_target_pairs={{0,1},{1,0},{2,3},{3,2},{4,5},{5,4},{6,7},{7,6},{8,9},{9,8},{10,11... | collective-permute-start | bytes 24584 | tf_op jit(solution)/shard_map/ppermute | solution.py:24
  233.3 14.7 %collective-permute-start.7 = (bf16[256,256]{1,0:T(8,128)(2,1)S(1)}, bf16[256,256]{1,0:T(8,128)(2,1)S(1)}, u32[]{:S(2)}, u32[]{:S(2)}) collective-permute-start(bf16[256,256]{1,0:T(8,128)(2,1)S(1)} %bitcast.330), channel_id=1, source_target_pairs={{0,3},{1,2},{2,1},{3,0},{4,7},{5,6},{6,5},{7,4},{8,11},{9,10},{10,... | collective-permute-start | bytes 393224 | tf_op jit(solution)/shard_map/ppermute | solution.py:24
  237.3 10.7 %collective-permute-start.6 = (bf16[256,256]{1,0:T(8,128)(2,1)S(1)}, bf16[256,256]{1,0:T(8,128)(2,1)}, u32[]{:S(2)}, u32[]{:S(2)}) collective-permute-start(bf16[256,256]{1,0:T(8,128)(2,1)S(1)} %bitcast.329), channel_id=1, source_target_pairs={{0,2},{1,3},{2,0},{3,1},{4,6},{5,7},{6,4},{7,5},{8,10},{9,11},{10,... | collective-permute-start | bytes 393224 | tf_op jit(solution)/shard_map/ppermute | solution.py:24
  238.0 8.8 %collective-permute-start.12 = (f32[2,1024]{1,0:T(2,128)S(1)}, f32[2,1024]{1,0:T(2,128)}, u32[]{:S(2)}, u32[]{:S(2)}) collective-permute-start(f32[2,1024]{1,0:T(2,128)S(1)} %add.376), channel_id=1, source_target_pairs={{0,2},{1,3},{2,0},{3,1},{4,6},{5,7},{6,4},{7,5},{8,10},{9,11},{10,... | collective-permute-start | bytes 24584 | tf_op jit(solution)/shard_map/ppermute | solution.py:24
  246.7 5.0 %collective-permute-start.5 = (bf16[256,256]{1,0:T(8,128)(2,1)S(1)}, bf16[256,256]{1,0:T(8,128)(2,1)S(1)}, u32[]{:S(2)}, u32[]{:S(2)}) collective-permute-start(bf16[256,256]{1,0:T(8,128)(2,1)S(1)} %bitcast.331), channel_id=1, source_target_pairs={{0,1},{1,0},{2,3},{3,2},{4,5},{5,4},{6,7},{7,6},{8,9},{9,8},{10,11... | collective-permute-start | bytes 393224 | tf_op jit(solution)/shard_map/ppermute | solution.py:24
  248.0 20.8 %collective-permute-start.23 = (bf16[512,256]{1,0:T(8,128)(2,1)S(1)}, bf16[512,256]{1,0:T(8,128)(2,1)}, u32[]{:S(2)}, u32[]{:S(2)}) collective-permute-start(bf16[512,256]{1,0:T(8,128)(2,1)S(1)} %bitcast.322), channel_id=1, source_target_pairs={{0,4},{4,0},{8,12},{12,8},{16,20},{20,16},{24,28},{28,24},{1,5},{5... | collective-permute-start | bytes 786440 | tf_op jit(solution)/shard_map/ppermute | solution.py:24
  248.0 25.8 %collective-permute-start.33 = (bf16[512,1024]{0,1:T(8,128)(2,1)}, bf16[512,1024]{0,1:T(8,128)(2,1)}, u32[]{:S(2)}, u32[]{:S(2)}) collective-permute-start(bf16[512,1024]{0,1:T(8,128)(2,1)} %pad_maximum_fusion.6), channel_id=1, source_target_pairs={{0,4},{4,0},{8,12},{12,8},{16,20},{20,16},{24,28},{28,24},{1,5},{5... | collective-permute-start | bytes 3145736 | tf_op jit(solution)/shard_map/ppermute | solution.py:24
  251.7 29.4 %collective-permute-start.35 = (bf16[512,1024]{0,1:T(8,128)(2,1)}, bf16[512,1024]{0,1:T(8,128)(2,1)}, u32[]{:S(2)}, u32[]{:S(2)}) collective-permute-start(bf16[512,1024]{0,1:T(8,128)(2,1)} %pad_maximum_fusion.7), channel_id=1, source_target_pairs={{0,4},{4,0},{8,12},{12,8},{16,20},{20,16},{24,28},{28,24},{1,5},{5... | collective-permute-start | bytes 3145736 | tf_op jit(solution)/shard_map/ppermute | solution.py:24
  266.5 35.2 %collective-permute-start.18 = (bf16[2,2,128,384]{3,2,1,0:T(8,128)(2,1)}, bf16[2,2,128,384]{3,2,1,0:T(8,128)(2,1)}, u32[]{:S(2)}, u32[]{:S(2)}) collective-permute-start(bf16[2,2,128,384]{3,2,1,0:T(8,128)(2,1)} %fusion.70), channel_id=1, source_target_pairs={{0,16},{4,20},{8,24},{12,28},{16,0},{20,4},{24,8},{28,12},{1,17},{... | collective-permute-start | bytes 1179656 | tf_op jit(solution)/shard_map/ppermute | solution.py:24
  268.8 35.1 %collective-permute-start.15 = (bf16[2,2,128,384]{3,2,1,0:T(8,128)(2,1)}, bf16[2,2,128,384]{3,2,1,0:T(8,128)(2,1)S(1)}, u32[]{:S(2)}, u32[]{:S(2)}) collective-permute-start(bf16[2,2,128,384]{3,2,1,0:T(8,128)(2,1)} %fusion.71), channel_id=1, source_target_pairs={{0,8},{4,12},{8,0},{12,4},{16,24},{20,28},{24,16},{28,20},{1,9},{5... | collective-permute-start | bytes 1179656 | tf_op jit(solution)/shard_map/ppermute | solution.py:24
  272.6 32.9 %collective-permute-start.28 = (bf16[2,2,32,512]{3,2,1,0:T(8,128)(2,1)}, bf16[2,2,32,512]{3,2,1,0:T(8,128)(2,1)}, u32[]{:S(2)}, u32[]{:S(2)}) collective-permute-start(bf16[2,2,32,512]{3,2,1,0:T(8,128)(2,1)} %fusion.83), channel_id=1, source_target_pairs={{0,16},{4,20},{8,24},{12,28},{16,0},{20,4},{24,8},{28,12},{1,17},{... | collective-permute-start | bytes 393224 | tf_op jit(solution)/shard_map/ppermute | solution.py:24
  273.8 33.7 %collective-permute-start.25 = (bf16[2,2,32,512]{3,2,1,0:T(8,128)(2,1)}, bf16[2,2,32,512]{3,2,1,0:T(8,128)(2,1)}, u32[]{:S(2)}, u32[]{:S(2)}) collective-permute-start(bf16[2,2,32,512]{3,2,1,0:T(8,128)(2,1)} %fusion.82), channel_id=1, source_target_pairs={{0,8},{4,12},{8,0},{12,4},{16,24},{20,28},{24,16},{28,20},{1,9},{5... | collective-permute-start | bytes 393224 | tf_op jit(solution)/shard_map/ppermute | solution.py:24
  295.0 68.5 %collective-permute-start.39 = (bf16[2,2,128,512]{3,2,1,0:T(8,128)(2,1)S(1)}, bf16[2,2,128,512]{3,2,1,0:T(8,128)(2,1)S(1)}, u32[]{:S(2)}, u32[]{:S(2)}) collective-permute-start(bf16[2,2,128,512]{3,2,1,0:T(8,128)(2,1)S(1)} %fusion.56), channel_id=1, source_target_pairs={{0,16},{4,20},{8,24},{12,28},{16,0},{20,4},{24,8},{28,12},{1,17},{... | collective-permute-start | bytes 1572872 | tf_op jit(solution)/shard_map/ppermute | solution.py:24
  301.7 64.7 %collective-permute-start.36 = (bf16[2,2,128,512]{3,2,1,0:T(8,128)(2,1)S(1)}, bf16[2,2,128,512]{3,2,1,0:T(8,128)(2,1)S(1)}, u32[]{:S(2)}, u32[]{:S(2)}) collective-permute-start(bf16[2,2,128,512]{3,2,1,0:T(8,128)(2,1)S(1)} %fusion.59), channel_id=1, source_target_pairs={{0,8},{4,12},{8,0},{12,4},{16,24},{20,28},{24,16},{28,20},{1,9},{5... | collective-permute-start | bytes 1572872 | tf_op jit(solution)/shard_map/ppermute | solution.py:24
  303.9 65.5 %collective-permute-start.47 = (bf16[2,2,128,512]{3,2,1,0:T(8,128)(2,1)S(1)}, bf16[2,2,128,512]{3,2,1,0:T(8,128)(2,1)S(1)}, u32[]{:S(2)}, u32[]{:S(2)}) collective-permute-start(bf16[2,2,128,512]{3,2,1,0:T(8,128)(2,1)S(1)} %fusion.58), channel_id=1, source_target_pairs={{0,16},{4,20},{8,24},{12,28},{16,0},{20,4},{24,8},{28,12},{1,17},{... | collective-permute-start | bytes 1572872 | tf_op jit(solution)/shard_map/ppermute | solution.py:24
  305.5 36.4 %collective-permute-start.19 = (bf16[2,128,384]{2,1,0:T(8,128)(2,1)S(1)}, bf16[2,128,384]{2,1,0:T(8,128)(2,1)S(1)}, u32[]{:S(2)}, u32[]{:S(2)}) collective-permute-start(bf16[2,128,384]{2,1,0:T(8,128)(2,1)S(1)} %fusion.79), channel_id=1, source_target_pairs={{0,8},{4,12},{8,0},{12,4},{16,24},{20,28},{24,16},{28,20},{1,9},{5... | collective-permute-start | bytes 589832 | tf_op jit(solution)/shard_map/ppermute | solution.py:24
  307.5 13.0 %collective-permute-start.29 = (bf16[2,32,512]{2,1,0:T(8,128)(2,1)S(1)}, bf16[2,32,512]{2,1,0:T(8,128)(2,1)S(1)}, u32[]{:S(2)}, u32[]{:S(2)}) collective-permute-start(bf16[2,32,512]{2,1,0:T(8,128)(2,1)S(1)} %fusion.91), channel_id=1, source_target_pairs={{0,8},{4,12},{8,0},{12,4},{16,24},{20,28},{24,16},{28,20},{1,9},{5... | collective-permute-start | bytes 196616 | tf_op jit(solution)/shard_map/ppermute | solution.py:24
  320.5 4.3 %collective-permute-start.26 = (bf16[2,32,512]{2,1,0:T(8,128)(2,1)S(1)}, bf16[2,32,512]{2,1,0:T(8,128)(2,1)S(1)}, u32[]{:S(2)}, u32[]{:S(2)}) collective-permute-start(bf16[2,32,512]{2,1,0:T(8,128)(2,1)S(1)} %fusion.90), channel_id=1, source_target_pairs={{0,16},{4,20},{8,24},{12,28},{16,0},{20,4},{24,8},{28,12},{1,17},{... | collective-permute-start | bytes 196616 | tf_op jit(solution)/shard_map/ppermute | solution.py:24
  324.8 5.5 %collective-permute-start.30 = (bf16[32,512]{1,0:T(8,128)(2,1)S(1)}, bf16[32,512]{1,0:T(8,128)(2,1)S(1)}, u32[]{:S(2)}, u32[]{:S(2)}) collective-permute-start(bf16[32,512]{1,0:T(8,128)(2,1)S(1)} %fusion.95), channel_id=1, source_target_pairs={{0,2},{1,3},{2,0},{3,1},{4,6},{5,7},{6,4},{7,5},{8,10},{9,11},{10,... | collective-permute-start | bytes 98312 | tf_op jit(solution)/shard_map/ppermute | solution.py:24
  330.3 4.8 %collective-permute-start.27 = (bf16[32,512]{1,0:T(8,128)(2,1)S(1)}, bf16[32,512]{1,0:T(8,128)(2,1)S(1)}, u32[]{:S(2)}, u32[]{:S(2)}) collective-permute-start(bf16[32,512]{1,0:T(8,128)(2,1)S(1)} %fusion.94), channel_id=1, source_target_pairs={{0,2},{1,3},{2,0},{3,1},{4,6},{5,7},{6,4},{7,5},{8,10},{9,11},{10,... | collective-permute-start | bytes 98312 | tf_op jit(solution)/shard_map/ppermute | solution.py:24
  335.2 0.7 collective-permute-start.31
  335.9 34.5 %collective-permute-start.44 = (bf16[2,2,128,512]{3,2,1,0:T(8,128)(2,1)S(1)}, bf16[2,2,128,512]{3,2,1,0:T(8,128)(2,1)S(1)}, u32[]{:S(2)}, u32[]{:S(2)}) collective-permute-start(bf16[2,2,128,512]{3,2,1,0:T(8,128)(2,1)S(1)} %fusion.57), channel_id=1, source_target_pairs={{0,8},{4,12},{8,0},{12,4},{16,24},{20,28},{24,16},{28,20},{1,9},{5... | collective-permute-start | bytes 1572872 | tf_op jit(solution)/shard_map/ppermute | solution.py:24
  342.0 6.9 %collective-permute-start.16 = (bf16[2,128,384]{2,1,0:T(8,128)(2,1)S(1)}, bf16[2,128,384]{2,1,0:T(8,128)(2,1)S(1)}, u32[]{:S(2)}, u32[]{:S(2)}) collective-permute-start(bf16[2,128,384]{2,1,0:T(8,128)(2,1)S(1)} %fusion.78), channel_id=1, source_target_pairs={{0,16},{4,20},{8,24},{12,28},{16,0},{20,4},{24,8},{28,12},{1,17},{... | collective-permute-start | bytes 589832 | tf_op jit(solution)/shard_map/ppermute | solution.py:24
  348.9 5.5 %collective-permute-start.20 = (bf16[128,384]{1,0:T(8,128)(2,1)S(1)}, bf16[128,384]{1,0:T(8,128)(2,1)S(1)}, u32[]{:S(2)}, u32[]{:S(2)}) collective-permute-start(bf16[128,384]{1,0:T(8,128)(2,1)S(1)} %fusion.89), channel_id=1, source_target_pairs={{0,2},{1,3},{2,0},{3,1},{4,6},{5,7},{6,4},{7,5},{8,10},{9,11},{10,... | collective-permute-start | bytes 294920 | tf_op jit(solution)/shard_map/ppermute | solution.py:24
  354.4 5.5 %collective-permute-start.17 = (bf16[128,384]{1,0:T(8,128)(2,1)S(1)}, bf16[128,384]{1,0:T(8,128)(2,1)S(1)}, u32[]{:S(2)}, u32[]{:S(2)}) collective-permute-start(bf16[128,384]{1,0:T(8,128)(2,1)S(1)} %fusion.88), channel_id=1, source_target_pairs={{0,2},{1,3},{2,0},{3,1},{4,6},{5,7},{6,4},{7,5},{8,10},{9,11},{10,... | collective-permute-start | bytes 294920 | tf_op jit(solution)/shard_map/ppermute | solution.py:24
  360.0 10.7 %collective-permute-start.21 = (bf16[2,32,768]{2,1,0:T(8,128)(2,1)S(1)}, bf16[2,32,768]{2,1,0:T(8,128)(2,1)S(1)}, u32[]{:S(2)}, u32[]{:S(2)}) collective-permute-start(bf16[2,32,768]{2,1,0:T(8,128)(2,1)S(1)} %get-tuple-element.124), channel_id=1, source_target_pairs={{0,1},{1,0},{2,3},{3,2},{4,5},{5,4},{6,7},{7,6},{8,9},{9,8},{10,11... | collective-permute-start | bytes 294920 | tf_op jit(solution)/shard_map/ppermute | solution.py:24
  364.5 11.5 %collective-permute-start.40 = (bf16[2,128,512]{2,1,0:T(8,128)(2,1)}, bf16[2,128,512]{2,1,0:T(8,128)(2,1)}, u32[]{:S(2)}, u32[]{:S(2)}) collective-permute-start(bf16[2,128,512]{2,1,0:T(8,128)(2,1)} %fusion.73), channel_id=1, source_target_pairs={{0,8},{4,12},{8,0},{12,4},{16,24},{20,28},{24,16},{28,20},{1,9},{5... | collective-permute-start | bytes 786440 | tf_op jit(solution)/shard_map/ppermute | solution.py:24
  367.4 11.9 %collective-permute-start.37 = (bf16[2,128,512]{2,1,0:T(8,128)(2,1)}, bf16[2,128,512]{2,1,0:T(8,128)(2,1)}, u32[]{:S(2)}, u32[]{:S(2)}) collective-permute-start(bf16[2,128,512]{2,1,0:T(8,128)(2,1)} %fusion.72), channel_id=1, source_target_pairs={{0,16},{4,20},{8,24},{12,28},{16,0},{20,4},{24,8},{28,12},{1,17},{... | collective-permute-start | bytes 786440 | tf_op jit(solution)/shard_map/ppermute | solution.py:24
  370.4 10.9 %collective-permute-start.48 = (bf16[2,128,512]{2,1,0:T(8,128)(2,1)}, bf16[2,128,512]{2,1,0:T(8,128)(2,1)}, u32[]{:S(2)}, u32[]{:S(2)}) collective-permute-start(bf16[2,128,512]{2,1,0:T(8,128)(2,1)} %fusion.75), channel_id=1, source_target_pairs={{0,8},{4,12},{8,0},{12,4},{16,24},{20,28},{24,16},{28,20},{1,9},{5... | collective-permute-start | bytes 786440 | tf_op jit(solution)/shard_map/ppermute | solution.py:24
  370.7 1.7 collective-permute-start.22
  372.4 12.3 %collective-permute-start.45 = (bf16[2,128,512]{2,1,0:T(8,128)(2,1)}, bf16[2,128,512]{2,1,0:T(8,128)(2,1)}, u32[]{:S(2)}, u32[]{:S(2)}) collective-permute-start(bf16[2,128,512]{2,1,0:T(8,128)(2,1)} %fusion.74), channel_id=1, source_target_pairs={{0,16},{4,20},{8,24},{12,28},{16,0},{20,4},{24,8},{28,12},{1,17},{... | collective-permute-start | bytes 786440 | tf_op jit(solution)/shard_map/ppermute | solution.py:24
  377.0 18.6 %collective-permute-start.41 = (bf16[128,512]{1,0:T(8,128)(2,1)S(1)}, bf16[128,512]{1,0:T(8,128)(2,1)S(1)}, u32[]{:S(2)}, u32[]{:S(2)}) collective-permute-start(bf16[128,512]{1,0:T(8,128)(2,1)S(1)} %fusion.85), channel_id=1, source_target_pairs={{0,2},{1,3},{2,0},{3,1},{4,6},{5,7},{6,4},{7,5},{8,10},{9,11},{10,... | collective-permute-start | bytes 393224 | tf_op jit(solution)/shard_map/ppermute | solution.py:24
  380.5 17.9 %collective-permute-start.38 = (bf16[128,512]{1,0:T(8,128)(2,1)S(1)}, bf16[128,512]{1,0:T(8,128)(2,1)S(1)}, u32[]{:S(2)}, u32[]{:S(2)}) collective-permute-start(bf16[128,512]{1,0:T(8,128)(2,1)S(1)} %fusion.84), channel_id=1, source_target_pairs={{0,2},{1,3},{2,0},{3,1},{4,6},{5,7},{6,4},{7,5},{8,10},{9,11},{10,... | collective-permute-start | bytes 393224 | tf_op jit(solution)/shard_map/ppermute | solution.py:24
  382.4 18.9 %collective-permute-start.49 = (bf16[128,512]{1,0:T(8,128)(2,1)S(1)}, bf16[128,512]{1,0:T(8,128)(2,1)S(1)}, u32[]{:S(2)}, u32[]{:S(2)}) collective-permute-start(bf16[128,512]{1,0:T(8,128)(2,1)S(1)} %fusion.87), channel_id=1, source_target_pairs={{0,2},{1,3},{2,0},{3,1},{4,6},{5,7},{6,4},{7,5},{8,10},{9,11},{10,... | collective-permute-start | bytes 393224 | tf_op jit(solution)/shard_map/ppermute | solution.py:24
  385.7 20.1 %collective-permute-start.46 = (bf16[128,512]{1,0:T(8,128)(2,1)S(1)}, bf16[128,512]{1,0:T(8,128)(2,1)S(1)}, u32[]{:S(2)}, u32[]{:S(2)}) collective-permute-start(bf16[128,512]{1,0:T(8,128)(2,1)S(1)} %fusion.86), channel_id=1, source_target_pairs={{0,2},{1,3},{2,0},{3,1},{4,6},{5,7},{6,4},{7,5},{8,10},{9,11},{10,... | collective-permute-start | bytes 393224 | tf_op jit(solution)/shard_map/ppermute | solution.py:24
  398.5 7.2 %collective-permute-start.42 = (bf16[2,32,1024]{2,1,0:T(8,128)(2,1)S(1)}, bf16[2,32,1024]{2,1,0:T(8,128)(2,1)S(1)}, u32[]{:S(2)}, u32[]{:S(2)}) collective-permute-start(bf16[2,32,1024]{2,1,0:T(8,128)(2,1)S(1)} %get-tuple-element.116), channel_id=1, source_target_pairs={{0,1},{1,0},{2,3},{3,2},{4,5},{5,4},{6,7},{7,6},{8,9},{9,8},{10,11... | collective-permute-start | bytes 393224 | tf_op jit(solution)/shard_map/ppermute | solution.py:24
  405.8 1.4 collective-permute-start.43
  (52 other events, 315.8 us)
